TPU v7x, 128 devices: a whole 4x4x4 slice. The times are simulated.
128 devices in a mesh: fsdp: 32 (over z, x, y_hi), expert: 4 (over y_lo, core).
Axes of the slice: x: 4, y: 4 (y_hi: 2, y_lo: 2; y = y_hi * 2 + y_lo), z: 4, core: 2. Of those that a mesh axis runs over, the one named last changes fastest.
Arguments:
- tokens: bfloat16 [4096, 4096], P('fsdp'), may hold values from -6 to 6
- expert_ids: int32 [4096, 8], P('fsdp'), may hold values from 0 to 127, all different within a row; in each aligned block of 128 rows (0 to 127, 128 to 255, ...) at most 12 rows name the same one
- route_weights: float32 [4096, 8], P('fsdp'), may hold values from 0.1 to 1
- d_out: bfloat16 [4096, 4096], P('fsdp'), may hold values from -6 to 6
- gate_weight: bfloat16 [32, 4096, 1536], P('fsdp', None, 'expert'), may hold values from -0.09375 to 0.09375
- up_weight: bfloat16 [32, 4096, 1536], P('fsdp', None, 'expert'), may hold values from -0.09375 to 0.09375
- down_weight: bfloat16 [32, 1536, 4096], P('fsdp', 'expert'), may hold values from -0.15625 to 0.15625
Outputs:
- moe_out: bfloat16 [4096, 4096], P('fsdp')
- d_tokens: bfloat16 [4096, 4096], P('fsdp')
- d_route_weights: float32 [4096, 8], P('fsdp')
- d_gate_weight: bfloat16 [32, 4096, 1536], P('fsdp', None, 'expert')
- d_up_weight: bfloat16 [32, 4096, 1536], P('fsdp', None, 'expert')
- d_down_weight: bfloat16 [32, 1536, 4096], P('fsdp', 'expert')
Inputs may be any that keep to these rules, and one draw needn't show every extreme that they name: `expert_ids`: each row names 8 different experts. Among the rows of one block of 128 tokens no expert is named more than 12 times. Experts from 32 on are held elsewhere.
All inputs are finite; a program needn't handle non-finite values.
Results may differ from a plain program's by a relative error of at most 0.0065.
Values may be sent and summed in bfloat16 or wider, within the bound.
A program may use at most 128 MiB of HBM per device.

v0:
```python
import jax
import jax.numpy as jnp
from jax import lax
from jax.sharding import PartitionSpec as P

TOPK = 8
CAP = 12


def slot_table(route_ids, n_win, capacity):
    total_rows = route_ids.shape[0] * route_ids.shape[1]
    flat_ids = route_ids.reshape(total_rows)
    labels = jnp.arange(n_win, dtype=jnp.int32)
    onehot = (flat_ids[:, None] == labels[None, :]).astype(jnp.int32)
    rank_all = jnp.sum((jnp.cumsum(onehot, axis=0) - 1) * onehot, axis=1)
    inside = flat_ids < n_win
    slot_of = jnp.where(inside, flat_ids * capacity + rank_all, n_win * capacity)
    orders = jnp.arange(total_rows, dtype=jnp.int32)
    assign = jnp.zeros((n_win * capacity,), jnp.int32).at[slot_of].set(orders, mode="drop")
    filled = jnp.zeros((n_win * capacity,), jnp.float32).at[slot_of].set(1.0, mode="drop")
    return (slot_of, assign, filled)


def expert_pass(rows_in, cot_rows, w_gate, w_up, w_down):
    gate_pre = jnp.dot(rows_in, w_gate, preferred_element_type=jnp.float32)
    up_pre = jnp.dot(rows_in, w_up, preferred_element_type=jnp.float32)
    sigma = jax.nn.sigmoid(gate_pre)
    active = gate_pre * sigma
    hidden = (active * up_pre).astype(jnp.bfloat16)
    out_part = jnp.dot(hidden, w_down, preferred_element_type=jnp.float32)
    d_hidden = lax.dot_general(
        cot_rows, w_down, (((1,), (1,)), ((), ())), preferred_element_type=jnp.float32
    )
    slope = sigma * (1.0 + gate_pre * (1.0 - sigma))
    d_gate = (d_hidden * up_pre * slope).astype(jnp.bfloat16)
    d_up = (d_hidden * active).astype(jnp.bfloat16)
    dx_part = lax.dot_general(
        d_gate, w_gate, (((1,), (1,)), ((), ())), preferred_element_type=jnp.float32
    )
    dx_part = dx_part + lax.dot_general(
        d_up, w_up, (((1,), (1,)), ((), ())), preferred_element_type=jnp.float32
    )
    grad_gate = lax.dot_general(
        rows_in, d_gate, (((0,), (0,)), ((), ())), preferred_element_type=jnp.float32
    )
    grad_up = lax.dot_general(
        rows_in, d_up, (((0,), (0,)), ((), ())), preferred_element_type=jnp.float32
    )
    grad_down = lax.dot_general(
        hidden, cot_rows, (((0,), (0,)), ((), ())), preferred_element_type=jnp.float32
    )
    return (out_part, dx_part, grad_gate, grad_up, grad_down)


def run_experts(recv_rows, recv_cot, gate_weight, up_weight, down_weight, n_fsdp, held):
    width = recv_rows.shape[1]
    rows_four = recv_rows.reshape(n_fsdp, held, CAP, width)
    cot_four = recv_cot.reshape(n_fsdp, held, CAP, width)
    out_list, dx_list, gate_list, up_list, down_list = ([], [], [], [], [])
    out_part, dx_part, grad_gate, grad_up, grad_down = expert_pass(
        rows_four[:, 0].reshape(n_fsdp * CAP, width),
        cot_four[:, 0].reshape(n_fsdp * CAP, width),
        gate_weight[0],
        up_weight[0],
        down_weight[0],
    )
    out_list.append(out_part.reshape(n_fsdp, 1, CAP, width))
    dx_list.append(dx_part.reshape(n_fsdp, 1, CAP, width))
    gate_list.append(grad_gate.astype(jnp.bfloat16))
    up_list.append(grad_up.astype(jnp.bfloat16))
    down_list.append(grad_down.astype(jnp.bfloat16))
    out_parts = out_list[0].reshape(n_fsdp * held * CAP, width)
    dx_parts = dx_list[0].reshape(n_fsdp * held * CAP, width)
    return (out_parts, dx_parts, (jnp.stack(gate_list), jnp.stack(up_list), jnp.stack(down_list)))


def gather_back(ret_out, ret_dx, slot_of, weights, cot_block):
    n_slots = ret_out.shape[0]
    mask = (slot_of < n_slots).astype(jnp.float32)[:, None]
    index = jnp.minimum(slot_of, n_slots - 1)
    out_rows = ret_out[index].astype(jnp.float32) * mask
    dx_rows = ret_dx[index].astype(jnp.float32) * mask
    tok_rows, top = weights.shape
    moe_out = jnp.sum(
        (out_rows * weights.reshape(-1)[:, None]).reshape(tok_rows, top, -1), axis=1
    ).astype(jnp.bfloat16)
    d_tokens = jnp.sum(dx_rows.reshape(tok_rows, top, -1), axis=1).astype(jnp.bfloat16)
    d_route = jnp.sum(
        out_rows.reshape(tok_rows, top, -1) * cot_block.astype(jnp.float32)[:, None, :], axis=2
    )
    return (moe_out, d_tokens, d_route)


def per_device(tokens, expert_ids, route_weights, d_out, gate_weight, up_weight, down_weight):
    n_fsdp = lax.axis_size("fsdp")
    held = gate_weight.shape[0]
    n_win = n_fsdp * held
    slot_of, assign, filled = slot_table(expert_ids, n_win, CAP)
    source = assign // TOPK
    weight_flat = route_weights.reshape(-1)
    send_rows = tokens[source] * filled[:, None].astype(jnp.bfloat16)
    send_cot = (
        weight_flat[assign][:, None] * filled[:, None] * d_out[source].astype(jnp.float32)
    ).astype(jnp.bfloat16)
    recv_rows, recv_cot = (
        lax.all_to_all(send_rows, "fsdp", split_axis=0, concat_axis=0, tiled=True),
        lax.all_to_all(send_cot, "fsdp", split_axis=0, concat_axis=0, tiled=True),
    )
    out_parts, dx_parts, grads = run_experts(
        recv_rows, recv_cot, gate_weight, up_weight, down_weight, n_fsdp, held
    )
    out_sum, dx_sum = lax.psum((out_parts, dx_parts), "expert")
    ret_out, ret_dx = (
        lax.all_to_all(
            out_sum.astype(jnp.bfloat16), "fsdp", split_axis=0, concat_axis=0, tiled=True
        ),
        lax.all_to_all(
            dx_sum.astype(jnp.bfloat16), "fsdp", split_axis=0, concat_axis=0, tiled=True
        ),
    )
    moe_out, d_tokens, d_route = gather_back(ret_out, ret_dx, slot_of, route_weights, d_out)
    return (moe_out, d_tokens, d_route, grads[0], grads[1], grads[2])


def solution(mesh):
    in_specs = (
        P("fsdp", None),
        P("fsdp", None),
        P("fsdp", None),
        P("fsdp", None),
        P("fsdp", None, "expert"),
        P("fsdp", None, "expert"),
        P("fsdp", "expert", None),
    )
    out_specs = (
        P("fsdp", None),
        P("fsdp", None),
        P("fsdp", None),
        P("fsdp", None, "expert"),
        P("fsdp", None, "expert"),
        P("fsdp", "expert", None),
    )
    return jax.shard_map(
        per_device, mesh=mesh, in_specs=in_specs, out_specs=out_specs, check_vma=False
    )
```

profile of v0, /device:TPU:0, one launch (start us, length us, event | category | flops | bytes accessed | tf_op | source)
XLA Modules:
  0.0 598.6 jit_solution(1091442513330585390)
XLA Ops:
  2.4 9.0 %reduce-window.6 = s32[32,8,128]{2,1,0:T(8,128)S(1)} reduce-window(s32[32,8,128]{2,1,0:T(8,128)S(1)} %fusion.23, s32[]{:T(128)} %constant.13.clone.1), window={size=1x1x128 pad=0_0x0_0x127_0}, to_apply=%region_0.0 | reduce-window | flops 4161536 | bytes 262148 | tf_op jit(solution)/shard_map/reduce-window
  24.7 9.6 %gather_fusion.3 = bf16[384,4096]{1,0:T(8,128)(2,1)} fusion(bf16[128,4096]{1,0:T(8,128)(2,1)} %param.10, s32[1024]{0:T(1024)S(1)} %get-tuple-element.28), kind=kCustom, calls=%fused_computation.3 | custom fusion | bytes 6292992 | tf_op jit(solution)/shard_map/gather | solution.py:103
  34.3 6.0 reshape.183
  40.3 6.6 %multiply_convert_fusion = bf16[32,12,4096]{2,1,0:T(8,128)(2,1)} fusion(f32[32,12,4096]{2,1,0:T(8,128)} %reshape.183, f32[32,12]{1,0:T(8,128)S(1)} %mul.135), kind=kLoop, calls=%fused_computation.16 | loop fusion | flops 3145728 | bytes 9438720 | tf_op jit(solution)/shard_map/convert_element_type | solution.py:104
  46.8 11.3 %all-to-all-start.2 = ((bf16[32,12,4096]{2,1,0:T(8,128)(2,1)}), bf16[32,12,4096]{2,1,0:T(8,128)(2,1)}, u32[]{:S(2)}, u32[]{:S(2)}) async-start(bf16[32,12,4096]{2,1,0:T(8,128)(2,1)} %multiply_convert_fusion), calls=%async_computation.2 | async-start | bytes 8388608 | tf_op jit(solution)/shard_map/all_to_all | solution.py:107
  58.2 9.6 %gather_fusion = bf16[384,4096]{1,0:T(8,128)(2,1)} fusion(bf16[128,4096]{1,0:T(8,128)(2,1)} %param.7, s32[1024]{0:T(1024)S(1)} %get-tuple-element.28), kind=kCustom, calls=%fused_computation | custom fusion | bytes 6292992 | tf_op jit(solution)/shard_map/gather | solution.py:101
  67.8 5.5 gather.18
  77.8 36.8 %all-to-all-done.2 = bf16[32,12,4096]{2,1,0:T(8,128)(2,1)} async-done(((bf16[32,12,4096]{2,1,0:T(8,128)(2,1)}), bf16[32,12,4096]{2,1,0:T(8,128)(2,1)}, u32[]{:S(2)}, u32[]{:S(2)}) %all-to-all-start.2) | async-done | bytes 3145760 | tf_op jit(solution)/shard_map/all_to_all | solution.py:107
  114.6 6.6 %all-to-all-start = ((bf16[32,12,4096]{2,1,0:T(8,128)(2,1)}), bf16[32,12,4096]{2,1,0:T(8,128)(2,1)}, u32[]{:S(2)}, u32[]{:S(2)}) async-start(bf16[32,12,4096]{2,1,0:T(8,128)(2,1)} %broadcast_multiply_fusion), calls=%async_computation | async-start | bytes 8388608 | tf_op jit(solution)/shard_map/all_to_all | solution.py:106
  121.2 5.6 all_to_all.34
  126.8 5.5 fusion.9
  132.2 46.2 %all-to-all-done = bf16[32,12,4096]{2,1,0:T(8,128)(2,1)} async-done(((bf16[32,12,4096]{2,1,0:T(8,128)(2,1)}), bf16[32,12,4096]{2,1,0:T(8,128)(2,1)}, u32[]{:S(2)}, u32[]{:S(2)}) %all-to-all-start) | async-done | bytes 3145760 | tf_op jit(solution)/shard_map/all_to_all | solution.py:106
  178.5 5.6 all_to_all.29
  184.0 4.8 fusion.18
  201.7 216.8 %all-reduce.2 = (bf16[384,4096]{1,0:T(8,128)(2,1)S(1)}, bf16[384,4096]{1,0:T(8,128)(2,1)}) all-reduce(f32[384,4096]{1,0:T(8,128)} %convolution_add_fusion, f32[384,4096]{1,0:T(8,128)} %fusion.11), channel_id=1, replica_groups=mesh['fsdp'=32,'expert'=4] {'expert'}, use_global_device_ids=true, to_apply=%region_7.8 | all-reduce | flops 3145728 | bytes 18874368 | tf_op jit(solution)/shard_map/psum | solution.py:112
  418.5 5.5 all_to_all.30
  424.0 6.4 %all-to-all-start.1 = ((bf16[32,12,4096]{2,1,0:T(8,128)(2,1)}), bf16[32,12,4096]{2,1,0:T(8,128)(2,1)}, u32[]{:S(2)}, u32[]{:S(2)}) async-start(bf16[32,12,4096]{2,1,0:T(8,128)(2,1)} %all_to_all.30), calls=%async_computation.1 | async-start | bytes 8388608 | tf_op jit(solution)/shard_map/all_to_all | solution.py:114
  433.2 55.6 %all-to-all-done.1 = bf16[32,12,4096]{2,1,0:T(8,128)(2,1)} async-done(((bf16[32,12,4096]{2,1,0:T(8,128)(2,1)}), bf16[32,12,4096]{2,1,0:T(8,128)(2,1)}, u32[]{:S(2)}, u32[]{:S(2)}) %all-to-all-start.1) | async-done | bytes 3145760 | tf_op jit(solution)/shard_map/all_to_all | solution.py:114
  488.8 19.9 %all-to-all-start.3 = ((bf16[32,12,4096]{2,1,0:T(8,128)(2,1)}), bf16[32,12,4096]{2,1,0:T(8,128)(2,1)}, u32[]{:S(2)}, u32[]{:S(2)}) async-start(bf16[32,12,4096]{2,1,0:T(8,128)(2,1)} %all_to_all.35), calls=%async_computation.3 | async-start | bytes 8388608 | tf_op jit(solution)/shard_map/all_to_all | solution.py:117
  510.4 5.5 fusion.8
  527.6 7.8 %gather_fusion.1 = bf16[1024,4096]{1,0:T(8,128)(2,1)} fusion(bf16[384,4096]{1,0:T(8,128)(2,1)S(1)} %all_to_all.32, s32[1024]{0:T(1024)S(1)} %broadcast_clamp_fusion), kind=kCustom, calls=%fused_computation.1 | custom fusion | bytes 16781312 | tf_op jit(solution)/shard_map/gather | solution.py:81
  535.3 30.0 %all-to-all-done.3 = bf16[32,12,4096]{2,1,0:T(8,128)(2,1)} async-done(((bf16[32,12,4096]{2,1,0:T(8,128)(2,1)}), bf16[32,12,4096]{2,1,0:T(8,128)(2,1)}, u32[]{:S(2)}, u32[]{:S(2)}) %all-to-all-start.3) | async-done | bytes 3145760 | tf_op jit(solution)/shard_map/all_to_all | solution.py:117
  569.4 7.8 %gather_fusion.4 = bf16[1024,4096]{1,0:T(8,128)(2,1)} fusion(bf16[384,4096]{1,0:T(8,128)(2,1)S(1)} %all_to_all.37, s32[1024]{0:T(1024)S(1)} %broadcast_clamp_fusion), kind=kCustom, calls=%fused_computation.4 | custom fusion | bytes 16781312 | tf_op jit(solution)/shard_map/gather | solution.py:82
  577.1 17.6 %fusion.5 = (bf16[128,4096]{1,0:T(8,128)(2,1)}, bf16[128,4096]{1,0:T(8,128)(2,1)}) fusion(bf16[1024,4096]{1,0:T(8,128)(2,1)} %gather_fusion.4, f32[128,8]{1,0:T(8,128)S(1)} %get-tuple-element.16, f32[128,8]{1,0:T(8,128)S(1)} %copy-done.10, bf16[1024,4096]{1,0:T(8,128)(2,1)} %gather_fusion.1), kind=kLoop, calls=%fused_computation.15 | loop fusion | flops 28311552 | bytes 18882560 | tf_op jit(solution)/shard_map/reduce_sum | solution.py:87
  (77 shorter events, 56.0 us)
Async XLA Ops:
  0.6 188.2 %copy-start = (bf16[1,4096,384]{2,1,0:T(8,128)(2,1)S(1)}, bf16[1,4096,384]{2,1,0:T(8,128)(2,1)}, u32[]{:S(2)}) copy-start(bf16[1,4096,384]{2,1,0:T(8,128)(2,1)} %param.12) | copy-start | bytes 9437188
  18.3 16.0 %copy-start.9 = (f32[128,8]{1,0:T(8,128)}, f32[128,8]{1,0:T(8,128)S(1)}, u32[]{:S(2)}) copy-start(f32[128,8]{1,0:T(8,128)S(1)} %copy.21) | copy-start | bytes 12292
  46.8 67.7 %all-to-all-start.2 = ((bf16[32,12,4096]{2,1,0:T(8,128)(2,1)}), bf16[32,12,4096]{2,1,0:T(8,128)(2,1)}, u32[]{:S(2)}, u32[]{:S(2)}) async-start(bf16[32,12,4096]{2,1,0:T(8,128)(2,1)} %multiply_convert_fusion), calls=%async_computation.2 | async-start | bytes 8388608 | tf_op jit(solution)/shard_map/all_to_all | solution.py:107
  114.6 63.9 %all-to-all-start = ((bf16[32,12,4096]{2,1,0:T(8,128)(2,1)}), bf16[32,12,4096]{2,1,0:T(8,128)(2,1)}, u32[]{:S(2)}, u32[]{:S(2)}) async-start(bf16[32,12,4096]{2,1,0:T(8,128)(2,1)} %broadcast_multiply_fusion), calls=%async_computation | async-start | bytes 8388608 | tf_op jit(solution)/shard_map/all_to_all | solution.py:106
  184.0 4.8 copy-start.5
  184.0 4.8 copy-start.15
  188.8 2.0 copy-start.7
  190.8 1.9 copy-start.13
  190.8 1.9 copy-start.11
  192.7 4.5 copy-start.8
  424.0 64.8 %all-to-all-start.1 = ((bf16[32,12,4096]{2,1,0:T(8,128)(2,1)}), bf16[32,12,4096]{2,1,0:T(8,128)(2,1)}, u32[]{:S(2)}, u32[]{:S(2)}) async-start(bf16[32,12,4096]{2,1,0:T(8,128)(2,1)} %all_to_all.30), calls=%async_computation.1 | async-start | bytes 8388608 | tf_op jit(solution)/shard_map/all_to_all | solution.py:114
  433.2 75.5 %copy-start.2 = (bf16[128,4096]{1,0:T(8,128)(2,1)S(1)}, bf16[128,4096]{1,0:T(8,128)(2,1)}, u32[]{:S(2)}) copy-start(bf16[128,4096]{1,0:T(8,128)(2,1)} %param.10) | copy-start | bytes 3145732
  488.8 76.5 %all-to-all-start.3 = ((bf16[32,12,4096]{2,1,0:T(8,128)(2,1)}), bf16[32,12,4096]{2,1,0:T(8,128)(2,1)}, u32[]{:S(2)}, u32[]{:S(2)}) async-start(bf16[32,12,4096]{2,1,0:T(8,128)(2,1)} %all_to_all.35), calls=%async_computation.3 | async-start | bytes 8388608 | tf_op jit(solution)/shard_map/all_to_all | solution.py:117
  510.4 5.6 copy-start.6
  510.4 5.5 copy-start.14
  516.0 3.8 copy-start.12
  569.3 7.8 %copy-start.10 = (f32[128,8]{1,0:T(8,128)S(1)}, f32[128,8]{1,0:T(8,128)}, u32[]{:S(2)}) copy-start(f32[128,8]{1,0:T(8,128)} %copy-done.9) | copy-start | bytes 12292
  577.1 17.6 %copy-start.3 = (bf16[1024,4096]{1,0:T(8,128)(2,1)S(1)}, bf16[1024,4096]{1,0:T(8,128)(2,1)}, u32[]{:S(2)}) copy-start(bf16[1024,4096]{1,0:T(8,128)(2,1)} %gather_fusion.1) | copy-start | bytes 25165828
  577.1 17.6 %copy-start.4 = (f32[128,4096]{1,0:T(8,128)S(1)}, f32[128,4096]{1,0:T(8,128)}, u32[]{:S(2)}) copy-start(f32[128,4096]{1,0:T(8,128)} %convert_element_type.98) | copy-start | bytes 6291460
  577.1 21.3 %copy-start.1 = (bf16[1,4096,384]{2,1,0:T(8,128)(2,1)S(1)}, bf16[1,4096,384]{2,1,0:T(8,128)(2,1)}, u32[]{:S(2)}) copy-start(bf16[1,4096,384]{2,1,0:T(8,128)(2,1)} %param.12) | copy-start | bytes 9437188
where the time goes:
time: 607 us; the launch traced here: 599 us
  blocking collectives  217 us (36%)
  waiting for transfers between devices  169 us (28%)
  local copies, waits for them, and re-layouts  88.6 us (15%)
  starting transfers between devices  44.2 us (7%)
  other arithmetic  43 us (7%)
  matrix products  36.2 us (6%)
    psum x1, blocking collectives, per_device(): out_sum, dx_sum = lax.psum((out_parts, dx_parts), 'expert')  217 us
    all_to_all x1, waiting for transfers between devices, per_device(): lax.all_to_all(out_sum.astype(jnp.bfloat16), 'fsdp', split_axis=0, concat...  55.6 us
    all_to_all x1, waiting for transfers between devices, per_device(): lax.all_to_all(send_rows, 'fsdp', split_axis=0, concat_axis=0, tiled=True)  46.2 us
    all_to_all x1, waiting for transfers between devices, per_device(): lax.all_to_all(send_cot, 'fsdp', split_axis=0, concat_axis=0, tiled=True)  36.8 us
    all_to_all x1, waiting for transfers between devices, per_device(): lax.all_to_all(dx_sum.astype(jnp.bfloat16), 'fsdp', split_axis=0, concat_...  30 us
    all_to_all x1, starting transfers between devices, per_device(): lax.all_to_all(dx_sum.astype(jnp.bfloat16), 'fsdp', split_axis=0, concat_...  19.9 us
    reduce_sum x1, other arithmetic, gather_back(): jnp.sum(dx_rows.reshape(tok_rows, top, -1), axis=1).astype(jnp.bfloat16)  17.6 us
    gather x2, local copies, waits for them, and re-layouts, per_device(): send_rows = tokens[source] * filled[:, None].astype(jnp.bfloat16)  15.1 us
  transfers between devices with their start and end apart: 4, of which 4 were waited for; matrix products, arithmetic and copies ran while one was open for 8% of the time, Pallas kernels for 0%

commit v1 on v0

v1 whole, which is shorter than its diff:
```python
import jax
import jax.numpy as jnp
from jax import lax
from jax.experimental import pallas as pl
from jax.experimental.pallas import tpu as pltpu
from jax.sharding import PartitionSpec as P

MESH = pl.DeviceIdType.MESH
BF = jnp.bfloat16
F32 = jnp.float32

D = 4096
FH = 384
SRC = 32
TOK = 128
CAP = 12
ROWS = SRC * CAP
W = 512
MSG = 4 * CAP
Q = W // 4
HALF = D // 2
NP = HALF // W


def dot(a, b):
    return lax.dot_general(a, b, (((1,), (0,)), ((), ())), preferred_element_type=F32)


def dot_nt(a, b):
    return lax.dot_general(a, b, (((1,), (1,)), ((), ())), preferred_element_type=F32)


def dot_tn(a, b):
    return lax.dot_general(a, b, (((0,), (0,)), ((), ())), preferred_element_type=F32)


def iota(shape, dim):
    return lax.broadcasted_iota(jnp.int32, shape, dim)


def part_and_rank(m):
    part = (
        (m >= CAP).astype(jnp.int32)
        + (m >= 2 * CAP).astype(jnp.int32)
        + (m >= 3 * CAP).astype(jnp.int32)
    )
    return part, m - CAP * part


def over_msg(j):
    return (j * 1366) >> 16


def spread(i, f):
    a, b, c = i % 4, (i // 4) % 4, i // 16
    dz, dx, dy = a, (a + b) % 4, (a + b + c) % 2
    z, x, y = f // 8, (f // 2) % 4, f % 2
    return ((z + dz) % 4) * 8 + ((x + dx) % 4) * 2 + (y + dy) % 2


def wait_bytes(ref, sem):
    pltpu.make_async_copy(ref, ref, sem).wait()


def kernel(
    ids_ref, w_ref, tok_hbm, dout_hbm, gate_hbm, up_hbm, down_hbm,
    moe_hbm, dtok_hbm, droute_ref, dgate_hbm, dup_hbm, ddown_hbm,
    tok_v, dout_v, code_s, wt_s, e_s, gs_s, et_s, whi_s, wlo_s, rhs_s, pm_s,
    s_s, r_s, xg_s, gu_s, dn_s, gu_acc, dh_acc, hid_s, dgu_s,
    xo_s, xi_s, v_s, sr_s, rr_s, acc_s, dq_s, mq_s, dr_s,
    tok_sem, w_sem, ssem, rsem, lsem, fs_sem, fr_sem,
    xs_sem, xr_sem, s2_sem, r2_sem, l2_sem, g_sem,
    ms_sem, mr_sem, ys_sem, yr_sem, hs_sem, hr_sem, ds_sem, dr_sem, o_sem,
):
    f = lax.axis_index("fsdp")
    e = lax.axis_index("expert")
    y, c = e // 2, e % 2
    mate = e + 1 - 2 * c
    other = (e + 2) % 4
    diag = (mate + 2) % 4

    bar = pltpu.get_barrier_semaphore()

    def greet(i, carry):
        f2 = spread(i, f)

        @pl.when(i > 0)
        def _():
            pl.semaphore_signal(bar, inc=1, device_id=(f2, e), device_id_type=MESH)

        pl.semaphore_signal(bar, inc=1, device_id=(f2, other), device_id_type=MESH)
        return carry

    lax.fori_loop(0, SRC, greet, 0)
    pl.semaphore_signal(bar, inc=1, device_id=(f, mate), device_id_type=MESH)
    pl.semaphore_signal(bar, inc=1, device_id=(f, diag), device_id_type=MESH)

    half = pl.ds(pl.multiple_of(c * HALF, HALF), HALF)
    tok_in = pltpu.make_async_copy(tok_hbm.at[:, half], tok_v, tok_sem.at[0])
    dout_in = pltpu.make_async_copy(dout_hbm.at[:, half], dout_v, tok_sem.at[1])
    tok_in.start()
    dout_in.start()
    for j in range(2 * NP):
        cols = pl.ds(j * W, W)
        pltpu.make_async_copy(gate_hbm.at[0, cols, :], gu_s.at[j, :, pl.ds(0, FH)], w_sem.at[0]).start()
        pltpu.make_async_copy(up_hbm.at[0, cols, :], gu_s.at[j, :, pl.ds(FH, FH)], w_sem.at[0]).start()
        pltpu.make_async_copy(down_hbm.at[0, :, cols], dn_s.at[j], w_sem.at[1]).start()

    ids = ids_ref[...]
    wts = w_ref[...]
    lane = iota((TOK, 128), 1)
    named = jnp.zeros((TOK, 128), F32)
    wmat = jnp.zeros((TOK, 128), F32)
    for k in range(ids.shape[1]):
        hit = ids[:, k : k + 1] == lane
        named = named + jnp.where(hit, 1.0, 0.0)
        wmat = wmat + jnp.where(hit, wts[:, k : k + 1], 0.0)
    earlier = jnp.where(lane < iota((TOK, 128), 0), 1.0, 0.0).astype(BF)
    code = jnp.where(named > 0.5, dot(earlier, named.astype(BF)) + 1.0, 0.0)
    code_s[...] = code.T
    wt_s[...] = wmat.T

    m48 = iota((MSG, TOK), 0)
    part48, rank48 = part_and_rank(m48)
    want48 = (rank48 + 1).astype(F32)

    def build_e(n, carry):
        hit = code_s[pl.ds(n, 1), :] == want48
        scale = jnp.sum(jnp.where(hit, wt_s[pl.ds(n, 1), :], 0.0), axis=1, keepdims=True)
        gs_s[n] = jnp.broadcast_to(scale, (MSG, TOK))
        for q in range(4):
            e_s[n, :, q * TOK : (q + 1) * TOK] = jnp.where(hit & (part48 == q), 1.0, 0.0).astype(BF)
        return carry

    lax.fori_loop(0, SRC, build_e, 0)

    tok_in.wait()
    dout_in.wait()
    for p in range(NP):
        for q in range(4):
            cols = slice(p * W + q * Q, p * W + (q + 1) * Q)
            rhs_s[q * TOK : (q + 1) * TOK, 0:Q] = tok_v[:, cols]
            rhs_s[q * TOK : (q + 1) * TOK, Q : 2 * Q] = dout_v[:, cols]

        def pack(g, carry, p=p):
            some = pl.ds(g * 4, 4)
            rows = dot(e_s[some].reshape(4 * MSG, 4 * TOK), rhs_s[...])
            cot = rows[:, Q:] * gs_s[some].reshape(4 * MSG, TOK)
            s_s[p, some, 0:MSG, :] = rows[:, :Q].astype(BF).reshape(4, MSG, Q)
            s_s[p, some, MSG : 2 * MSG, :] = cot.astype(BF).reshape(4, MSG, Q)
            return carry

        lax.fori_loop(0, SRC // 4, pack, 0)
        if p == 0:
            pl.semaphore_wait(bar, 2 * SRC + 1)

        def send(i, carry, p=p):
            f2 = spread(i, f)
            e2 = (e + 2 * ((f + f2) % 2)) % 4
            pltpu.make_async_remote_copy(
                s_s.at[p, f2], r_s.at[p, f], ssem.at[p], rsem.at[p],
                device_id=(f2, e2), device_id_type=MESH,
            ).start()
            return carry

        lax.fori_loop(1, SRC, send, 0)
        pltpu.make_async_copy(s_s.at[p, f], r_s.at[p, f], lsem.at[p]).start()

    i_p = iota((4 * MSG, 4 * MSG), 0)
    q_p = over_msg(i_p)
    s_p, r_p = part_and_rank(i_p - MSG * q_p)
    pm_s[...] = jnp.where(iota((4 * MSG, 4 * MSG), 1) == MSG * s_p + CAP * q_p + r_p, 1.0, 0.0).astype(BF)

    w_hi = wmat.astype(BF)
    w_lo = (wmat - w_hi.astype(F32)).astype(BF)
    code_b = code.astype(BF)

    def build_et(g, carry):
        j = iota((TOK, 8 * MSG), 1)
        n = over_msg(j)
        part, rank = part_and_rank(j - MSG * n)
        rep = jnp.where(iota((TOK, 8 * MSG), 0) == n + 8 * g, 1.0, 0.0).astype(BF)
        hit = dot(code_b, rep) == (rank + 1).astype(F32)
        hi = dot(w_hi, rep)
        lo = dot(w_lo, rep)
        for q in range(4):
            here = hit & (part == q)
            rows = slice(q * TOK, (q + 1) * TOK)
            et_s[g, rows, :] = jnp.where(here, 1.0, 0.0).astype(BF)
            whi_s[g, rows, :] = jnp.where(here, hi, 0.0).astype(BF)
            wlo_s[g, rows, :] = jnp.where(here, lo, 0.0).astype(BF)
        return carry

    lax.fori_loop(0, 4, build_et, 0)
    for pp in range(2):
        for q in range(4):
            cols = pl.ds(pl.multiple_of(y * (HALF // 2) + pp * W + q * Q, Q), Q)
            dq_s[q * TOK : (q + 1) * TOK, pp * Q : (pp + 1) * Q] = dout_v[:, cols]
    gu_acc[...] = jnp.zeros_like(gu_acc)
    dh_acc[...] = jnp.zeros_like(dh_acc)
    wait_bytes(gu_s, w_sem.at[0])
    wait_bytes(dn_s, w_sem.at[1])

    def first(j):
        for n in range(3):
            cols = slice(n * 256, (n + 1) * 256)
            gu_acc[:, cols] += dot(xg_s[j, 0], gu_s[j, :, cols])
        dh_acc[...] += dot_nt(xg_s[j, 1], dn_s[j])

    def arrive(p, carry):
        mine = c * NP + p
        theirs = (1 - c) * NP + p
        wait_bytes(r_s.at[p, pl.ds(0, SRC - 1)], rsem.at[p])
        pltpu.make_async_copy(s_s.at[p, f], r_s.at[p, f], lsem.at[p]).wait()

        def unpack(g, carry):
            some = pl.ds(g * 4, 4)
            rows = pl.ds(pl.multiple_of(g * MSG, MSG), MSG)
            x = r_s[p, some, 0:MSG, :].reshape(4 * MSG, Q)
            ct = r_s[p, some, MSG : 2 * MSG, :].reshape(4 * MSG, Q)
            out = dot(pm_s[...], jnp.concatenate([x, ct], axis=1)).astype(BF)
            for q in range(4):
                xg_s[mine, 0, rows, q * Q : (q + 1) * Q] = out[q * MSG : (q + 1) * MSG, :Q]
                xg_s[mine, 1, rows, q * Q : (q + 1) * Q] = out[q * MSG : (q + 1) * MSG, Q:]
            return carry

        lax.fori_loop(0, SRC // 4, unpack, 0)
        pltpu.make_async_remote_copy(
            xg_s.at[mine], xg_s.at[mine], fs_sem.at[p], fr_sem.at[p],
            device_id=(f, mate), device_id_type=MESH,
        ).start()
        first(mine)
        wait_bytes(xg_s.at[theirs], fr_sem.at[p])
        first(theirs)
        return carry

    lax.fori_loop(0, NP, arrive, 0)

    def middle(n, carry):
        rows = pl.ds(pl.multiple_of(n * 96, 96), 96)
        gate = gu_acc[rows, 0:FH]
        up = gu_acc[rows, FH : 2 * FH]
        dh = dh_acc[rows, :]
        sig = jax.nn.sigmoid(gate)
        act = gate * sig
        hid_s[rows, :] = (act * up).astype(BF)
        slope = sig * (1.0 + gate * (1.0 - sig))
        dgu_s[rows, 0:FH] = (dh * up * slope).astype(BF)
        dgu_s[rows, FH : 2 * FH] = (dh * act).astype(BF)
        return carry

    lax.fori_loop(0, ROWS // 96, middle, 0)

    def second(t, j):
        if t < 2:
            return dot(hid_s[...], dn_s[j])
        return dot_nt(dgu_s[...], gu_s[j])

    def for_mate(t):
        base = (1 - c) * NP + 2 * ((y + t % 2) % 2)

        def one(pp, carry):
            xo_s[t, pp] = second(t, base + pp).astype(BF)
            return carry

        lax.fori_loop(0, 2, one, 0)
        pltpu.make_async_remote_copy(
            xo_s.at[t], xi_s.at[t], xs_sem.at[t], xr_sem.at[t],
            device_id=(f, mate), device_id_type=MESH,
        ).start()

    def returned(t):
        dy = t % 2
        base = c * NP + 2 * ((y + dy) % 2)
        wait_bytes(xi_s.at[t], xr_sem.at[t])

        def one(pp, carry):
            v_s[pp] = (second(t, base + pp) + xi_s[t, pp].astype(F32)).astype(BF)
            return carry

        lax.fori_loop(0, 2, one, 0)

        def pack(g, carry):
            rows = pl.ds(pl.multiple_of(g * MSG, MSG), MSG)
            some = pl.ds(g * 4, 4)
            both = [
                jnp.concatenate([v_s[pp, rows, q * Q : (q + 1) * Q] for q in range(4)], axis=0)
                for pp in range(2)
            ]
            out = dot(pm_s[...], jnp.concatenate(both, axis=1)).astype(BF)
            for pp in range(2):
                sr_s[t, some, pp * MSG : (pp + 1) * MSG, :] = out[:, pp * Q : (pp + 1) * Q].reshape(4, MSG, Q)
            return carry

        lax.fori_loop(0, SRC // 4, pack, 0)
        e2 = other if dy else e

        def send(i, carry):
            f2 = spread(i, f)
            pltpu.make_async_remote_copy(
                sr_s.at[t, f2], rr_s.at[t, f], s2_sem.at[t], r2_sem.at[t],
                device_id=(f2, e2), device_id_type=MESH,
            ).start()
            return carry

        lax.fori_loop(1 - dy, SRC, send, 0)
        if dy == 0:
            pltpu.make_async_copy(sr_s.at[t, f], rr_s.at[t, f], l2_sem.at[t // 2]).start()

    for_mate(0)
    for_mate(1)
    returned(0)
    for_mate(2)
    returned(1)
    for_mate(3)
    returned(2)
    returned(3)

    for t in range(4):
        wait_bytes(xo_s.at[t], xs_sem.at[t])

    def grads(j, carry):
        cols = pl.ds(pl.multiple_of(j * W, W), W)
        for n in range(3):
            some = slice(n * 256, (n + 1) * 256)
            gu_s[j, :, some] = dot_tn(xg_s[j, 0], dgu_s[:, some]).astype(BF)
        pltpu.make_async_copy(gu_s.at[j, :, pl.ds(0, FH)], dgate_hbm.at[0, cols, :], g_sem.at[0]).start()
        pltpu.make_async_copy(gu_s.at[j, :, pl.ds(FH, FH)], dup_hbm.at[0, cols, :], g_sem.at[0]).start()
        dn_s[j] = dot_tn(hid_s[...], xg_s[j, 1]).astype(BF)
        pltpu.make_async_copy(dn_s.at[j], ddown_hbm.at[0, :, cols], g_sem.at[1]).start()
        return carry

    lax.fori_loop(0, 2 * NP, grads, 0)

    def rhs_of(t, g):
        some = pl.ds(g * 8, 8)
        return jnp.concatenate(
            [rr_s[t, some, pp * MSG : (pp + 1) * MSG, :].reshape(8 * MSG, Q) for pp in range(2)], axis=1
        )

    mine = 2 * c + y
    flip = 2 * c + 1 - y
    theirs = 2 * (1 - c) + y
    last = 2 * (1 - c) + 1 - y

    def landed(a):
        wait_bytes(rr_s.at[2 * a, pl.ds(0, SRC - 1)], r2_sem.at[2 * a])
        pltpu.make_async_copy(sr_s.at[2 * a, f], rr_s.at[2 * a, f], l2_sem.at[a]).wait()
        wait_bytes(rr_s.at[2 * a + 1], r2_sem.at[2 * a + 1])

    def share(a):
        for pp in range(2):
            for q in range(4):
                cols = slice(pp * W + q * Q, pp * W + (q + 1) * Q)
                mq_s[a, mine, :, cols] = acc_s[q * TOK : (q + 1) * TOK, pp * Q : (pp + 1) * Q].astype(BF)
        pltpu.make_async_remote_copy(
            mq_s.at[a, mine], mq_s.at[a, mine], ys_sem.at[a], yr_sem.at[a],
            device_id=(f, other), device_id_type=MESH,
        ).start()
        pltpu.make_async_remote_copy(
            mq_s.at[a, mine], mq_s.at[a, mine], ms_sem.at[a], mr_sem.at[a],
            device_id=(f, mate), device_id_type=MESH,
        ).start()

    def forward(a):
        wait_bytes(mq_s.at[a, flip], yr_sem.at[a])
        pltpu.make_async_remote_copy(
            mq_s.at[a, flip], mq_s.at[a, flip], hs_sem.at[a], hr_sem.at[a],
            device_id=(f, mate), device_id_type=MESH,
        ).start()

    def store(a, out_hbm):
        wait_bytes(mq_s.at[a, theirs], mr_sem.at[a])
        wait_bytes(mq_s.at[a, last], hr_sem.at[a])
        for n in range(4):
            pltpu.make_async_copy(mq_s.at[a, n], out_hbm.at[:, pl.ds(n * 1024, 1024)], o_sem.at[a]).start()

    landed(0)
    acc_s[...] = jnp.zeros_like(acc_s)
    dr_s[mine] = jnp.zeros((TOK, 128), F32)

    def combine_out(g, carry):
        a, b = rhs_of(0, g), rhs_of(1, g)
        acc_s[...] += dot(whi_s[g], a) + dot(whi_s[g], b) + dot(wlo_s[g], a) + dot(wlo_s[g], b)
        prod = dot_nt(dq_s[...], a) + dot_nt(dq_s[...], b)
        kept = jnp.where(et_s[g] > 0, prod, 0.0)
        total = kept[0:TOK] + kept[TOK : 2 * TOK] + kept[2 * TOK : 3 * TOK] + kept[3 * TOK :]
        hi = total.astype(BF)
        lo = (total - hi.astype(F32)).astype(BF)
        rep = jnp.where(
            iota((8 * MSG, 128), 1) == over_msg(iota((8 * MSG, 128), 0)) + 8 * g, 1.0, 0.0
        ).astype(BF)
        dr_s[mine] += dot(hi, rep) + dot(lo, rep)
        return carry

    lax.fori_loop(0, 4, combine_out, 0)
    share(0)
    for n, e2 in enumerate((mate, other, diag)):
        pltpu.make_async_remote_copy(
            dr_s.at[mine], dr_s.at[mine], ds_sem.at[n], dr_sem.at[n],
            device_id=(f, e2), device_id_type=MESH,
        ).start()
    forward(0)
    store(0, moe_hbm)
    for n, slot in enumerate((theirs, flip, last)):
        wait_bytes(dr_s.at[slot], dr_sem.at[n])
    total = dr_s[0] + dr_s[1] + dr_s[2] + dr_s[3]
    for k in range(ids.shape[1]):
        hit = ids[:, k : k + 1] == lane
        droute_ref[:, k : k + 1] = jnp.sum(jnp.where(hit, total, 0.0), axis=1, keepdims=True)

    landed(1)
    acc_s[...] = jnp.zeros_like(acc_s)

    def combine_dx(g, carry):
        acc_s[...] += dot(et_s[g], rhs_of(2, g)) + dot(et_s[g], rhs_of(3, g))
        return carry

    lax.fori_loop(0, 4, combine_dx, 0)
    share(1)
    forward(1)
    store(1, dtok_hbm)

    for p in range(NP):
        wait_bytes(s_s.at[p, pl.ds(0, SRC - 1)], ssem.at[p])
        wait_bytes(xg_s.at[0], fs_sem.at[p])
    for t in range(4):
        wait_bytes(sr_s.at[t, pl.ds(0, SRC - 1 + t % 2)], s2_sem.at[t])
    for n in range(3):
        wait_bytes(dr_s.at[0], ds_sem.at[n])
    for a in range(2):
        for sem in (ms_sem, ys_sem, hs_sem):
            wait_bytes(mq_s.at[a, 0], sem.at[a])
        wait_bytes(mq_s.at[a], o_sem.at[a])
    wait_bytes(gu_s, g_sem.at[0])
    wait_bytes(dn_s, g_sem.at[1])


def per_device(tokens, expert_ids, route_weights, d_out, gate_weight, up_weight, down_weight):
    hbm = pl.BlockSpec(memory_space=pl.ANY)
    vmem = pl.BlockSpec(memory_space=pltpu.VMEM)
    shape = jax.ShapeDtypeStruct
    dma = pltpu.SemaphoreType.DMA
    v = pltpu.VMEM
    return pl.pallas_call(
        kernel,
        out_shape=(
            shape((TOK, D), BF), shape((TOK, D), BF), shape(route_weights.shape, F32),
            shape(gate_weight.shape, BF), shape(up_weight.shape, BF), shape(down_weight.shape, BF),
        ),
        in_specs=[vmem, vmem, hbm, hbm, hbm, hbm, hbm],
        out_specs=(hbm, hbm, vmem, hbm, hbm, hbm),
        scratch_shapes=[
            v((TOK, HALF), BF), v((TOK, HALF), BF),
            v((128, TOK), F32), v((128, TOK), F32),
            v((SRC, MSG, 4 * TOK), BF), v((SRC, MSG, TOK), F32),
            v((4, 4 * TOK, 8 * MSG), BF), v((4, 4 * TOK, 8 * MSG), BF), v((4, 4 * TOK, 8 * MSG), BF),
            v((4 * TOK, 2 * Q), BF), v((4 * MSG, 4 * MSG), BF),
            v((NP, SRC, 2 * MSG, Q), BF), v((NP, SRC, 2 * MSG, Q), BF),
            v((2 * NP, 2, ROWS, W), BF),
            v((2 * NP, W, 2 * FH), BF), v((2 * NP, FH, W), BF),
            v((ROWS, 2 * FH), F32), v((ROWS, FH), F32),
            v((ROWS, FH), BF), v((ROWS, 2 * FH), BF),
            v((4, 2, ROWS, W), BF), v((4, 2, ROWS, W), BF), v((2, ROWS, W), BF),
            v((4, SRC, 2 * MSG, Q), BF), v((4, SRC, 2 * MSG, Q), BF),
            v((4 * TOK, 2 * Q), F32), v((4 * TOK, 2 * Q), BF),
            v((2, 4, TOK, D // 4), BF), v((4, TOK, 128), F32),
            dma((2,)), dma((2,)), dma((NP,)), dma((NP,)), dma((NP,)), dma((NP,)), dma((NP,)),
            dma((4,)), dma((4,)), dma((4,)), dma((4,)), dma((2,)), dma((2,)),
            dma((2,)), dma((2,)), dma((2,)), dma((2,)), dma((2,)), dma((2,)),
            dma((3,)), dma((3,)), dma((2,)),
        ],
        compiler_params=pltpu.CompilerParams(
            collective_id=0, has_side_effects=True, vmem_limit_bytes=60 * 1024 * 1024
        ),
        cost_estimate=pl.CostEstimate(flops=11_000_000_000, bytes_accessed=23_000_000, transcendentals=200_000),
    )(expert_ids, route_weights, tokens, d_out, gate_weight, up_weight, down_weight)


def solution(mesh):
    in_specs = (
        P("fsdp", None),
        P("fsdp", None),
        P("fsdp", None),
        P("fsdp", None),
        P("fsdp", None, "expert"),
        P("fsdp", None, "expert"),
        P("fsdp", "expert", None),
    )
    out_specs = (
        P("fsdp", None),
        P("fsdp", None),
        P("fsdp", None),
        P("fsdp", None, "expert"),
        P("fsdp", None, "expert"),
        P("fsdp", "expert", None),
    )
    return jax.shard_map(
        per_device, mesh=mesh, in_specs=in_specs, out_specs=out_specs, check_vma=False
    )
```

time: 607 us -> 135 us (0.22); the launches traced: 599 us -> 133 us
  blocking collectives: 217 us -> 0 us
  waiting for transfers between devices: 169 us -> 0 us
  Pallas kernels: 0 us -> 115 us
  local copies, waits for them, and re-layouts: 88.6 us -> 16.8 us
  starting transfers between devices: 44.2 us -> 0 us
  other arithmetic: 43 us -> 0 us
  matrix products: 36.2 us -> 0 us
    psum x1 -> x0, blocking collectives: 217 us -> none  [per_device(): out_sum, dx_sum = lax.psum((out_parts, dx_parts), 'expert')]
    all_to_all x4 -> x0, waiting for transfers between devices: 169 us -> none  [the longest x1 55.6 us: per_device(): lax.all_to_all(out_sum.astype(jnp.bfloat16), 'fsdp', split_axis=0, concat...]
    pallas_call x0 -> x1, Pallas kernels: none -> 115 us  [per_device(): pl.pallas_call(kernel, out_shape=(shape((TOK, D), BF), shape((TOK, D), BF...]
    all_to_all x4 -> x0, starting transfers between devices: 44.2 us -> none  [the longest x1 19.9 us: per_device(): lax.all_to_all(dx_sum.astype(jnp.bfloat16), 'fsdp', split_axis=0, concat_...]
    gather x6 -> x0, local copies, waits for them, and re-layouts: 42.1 us -> none  [the longest x2 15.1 us: per_device(): send_rows = tokens[source] * filled[:, None].astype(jnp.bfloat16)]
    dot_general x9 -> x0, matrix products: 36.2 us -> none  [the longest x1 5.53 us: expert_pass(): lax.dot_general(hidden, cot_rows, (((0,), (0,)), ((), ())), preferred_ele...]
    all_to_all x6 -> x0, local copies, waits for them, and re-layouts: 27.3 us -> none  [the longest x2 9.51 us: per_device(): lax.all_to_all(out_sum.astype(jnp.bfloat16), 'fsdp', split_axis=0, concat...]
    reduce_sum x3 -> x0, other arithmetic: 20.5 us -> none  [the longest x1 17.6 us: gather_back(): jnp.sum(dx_rows.reshape(tok_rows, top, -1), axis=1).astype(jnp.bfloat16)]
  transfers between devices with their start and end apart: 4 -> 0, of which waited for: 4 -> 0; matrix products, arithmetic and copies ran while one was open for 8% -> 0% of each run, Pallas kernels for 0% -> 0%
where the time goes in v1:
time: 135 us; the launch traced here: 133 us
  Pallas kernels  115 us (85%)
  local copies, waits for them, and re-layouts  16.8 us (12%)
    pallas_call x1, Pallas kernels, per_device(): pl.pallas_call(kernel, out_shape=(shape((TOK, D), BF), shape((TOK, D), BF...  115 us
    unnamed x13, local copies, waits for them, and re-layouts  15.1 us

profile of v1, /device:TPU:0, one launch (start us, length us, event | category | flops | bytes accessed | tf_op | source)
XLA Modules:
  0.0 132.7 jit_solution(17658878902868594376)
XLA Ops:
  0.6 1.4 %copy.13.ids_ref = s32[128,8]{1,0:T(8,128)} copy(s32[128,8]{0,1:T(8,128)} %param.8) | data formatting | bytes 8192 | tf_op args[1]
  2.0 1.4 %copy.14.w_ref = f32[128,8]{1,0:T(8,128)} copy(f32[128,8]{0,1:T(8,128)} %param.9) | data formatting | bytes 8192 | tf_op args[2]
  3.5 115.3 %shard_map.118 = (bf16[128,4096]{1,0:T(8,128)(2,1)}, bf16[128,4096]{1,0:T(8,128)(2,1)}, f32[128,8]{1,0:T(8,128)}, bf16[1,4096,384]{2,1,0:T(8,128)(2,1)}, bf16[1,...) custom-call(s32[128,8]{1,0:T(8,128)} %copy.13.ids_ref, f32[128,8]{1,0:T(8,128)} %copy.14.w_ref, ...), custom_call_target="tpu_custom_call" | custom-call | flops 11000000512 | bytes 23000000 | tf_op jit(solution)/shard_map/pallas_call | solution.py:445
  118.8 0.0 copy-start.2
  118.8 1.7 %copy.15 = f32[128,8]{0,1:T(8,128)} copy(f32[128,8]{1,0:T(8,128)} %get-tuple-element.8) | data formatting | bytes 8192 | tf_op jit(solution)/shard_map/pallas_call | solution.py:445
  120.4 2.3 %copy.21 = bf16[128,4096]{1,0:T(8,128)(2,1)} copy(bf16[128,4096]{1,0:T(8,128)(2,1)} %get-tuple-element.18) | data formatting | bytes 2097152
  122.7 2.3 %copy.22 = bf16[128,4096]{1,0:T(8,128)(2,1)} copy(bf16[128,4096]{1,0:T(8,128)(2,1)} %get-tuple-element.19) | data formatting | bytes 2097152
  125.0 0.0 copy-done.2
  125.0 0.0 copy-start.1
  125.0 1.7 %copy.23 = bf16[1,4096,384]{2,1,0:T(8,128)(2,1)} copy(bf16[1,4096,384]{2,1,0:T(8,128)(2,1)S(1)} %copy-done.2) | data formatting | bytes 6291456
  126.7 1.4 %copy-done.1 = bf16[1,4096,384]{2,1,0:T(8,128)(2,1)S(1)} copy-done((bf16[1,4096,384]{2,1,0:T(8,128)(2,1)S(1)}, bf16[1,4096,384]{2,1,0:T(8,128)(2,1)}, u32[]{:S(2)}) %copy-start.1) | copy-done | bytes 3145752
  128.0 0.0 copy-start
  128.0 1.7 %copy.24 = bf16[1,4096,384]{2,1,0:T(8,128)(2,1)} copy(bf16[1,4096,384]{2,1,0:T(8,128)(2,1)S(1)} %copy-done.1) | data formatting | bytes 6291456
  129.7 1.4 %copy-done = bf16[1,384,4096]{2,1,0:T(8,128)(2,1)S(1)} copy-done((bf16[1,384,4096]{2,1,0:T(8,128)(2,1)S(1)}, bf16[1,384,4096]{2,1,0:T(8,128)(2,1)}, u32[]{:S(2)}) %copy-start) | copy-done | bytes 3145752
  131.1 1.7 %copy.25 = bf16[1,384,4096]{2,1,0:T(8,128)(2,1)} copy(bf16[1,384,4096]{2,1,0:T(8,128)(2,1)S(1)} %copy-done) | data formatting | bytes 6291456
Async XLA Ops:
  118.8 6.2 %copy-start.2 = (bf16[1,4096,384]{2,1,0:T(8,128)(2,1)S(1)}, bf16[1,4096,384]{2,1,0:T(8,128)(2,1)}, u32[]{:S(2)}) copy-start(bf16[1,4096,384]{2,1,0:T(8,128)(2,1)} %get-tuple-element.21) | copy-start | bytes 9437188
  125.0 3.0 %copy-start.1 = (bf16[1,4096,384]{2,1,0:T(8,128)(2,1)S(1)}, bf16[1,4096,384]{2,1,0:T(8,128)(2,1)}, u32[]{:S(2)}) copy-start(bf16[1,4096,384]{2,1,0:T(8,128)(2,1)} %get-tuple-element.22) | copy-start | bytes 9437188
  128.0 3.0 %copy-start = (bf16[1,384,4096]{2,1,0:T(8,128)(2,1)S(1)}, bf16[1,384,4096]{2,1,0:T(8,128)(2,1)}, u32[]{:S(2)}) copy-start(bf16[1,384,4096]{2,1,0:T(8,128)(2,1)} %get-tuple-element.23) | copy-start | bytes 9437188

commit v2 on v1

v2 whole, which is shorter than its diff:
```python
import jax
import jax.numpy as jnp
from jax import lax
from jax.experimental import pallas as pl
from jax.experimental.pallas import tpu as pltpu
from jax.sharding import PartitionSpec as P

MESH = pl.DeviceIdType.MESH
BF = jnp.bfloat16
F32 = jnp.float32

D = 4096
FH = 384
SRC = 32
TOK = 128
CAP = 12
ROWS = SRC * CAP
W = 512
MSG = 4 * CAP
Q = W // 4
HALF = D // 2
NP = HALF // W


def dot(a, b):
    return lax.dot_general(a, b, (((1,), (0,)), ((), ())), preferred_element_type=F32)


def dot_nt(a, b):
    return lax.dot_general(a, b, (((1,), (1,)), ((), ())), preferred_element_type=F32)


def dot_tn(a, b):
    return lax.dot_general(a, b, (((0,), (0,)), ((), ())), preferred_element_type=F32)


def iota(shape, dim):
    return lax.broadcasted_iota(jnp.int32, shape, dim)


def part_and_rank(m):
    part = (
        (m >= CAP).astype(jnp.int32)
        + (m >= 2 * CAP).astype(jnp.int32)
        + (m >= 3 * CAP).astype(jnp.int32)
    )
    return part, m - CAP * part


def over_msg(j):
    return (j * 1366) >> 16


def step_from(f, dz, dx, dy):
    z, x, y = lax.div(f, 8), lax.rem(lax.div(f, 2), 4), lax.rem(f, 2)
    return lax.rem(z + dz, 4) * 8 + lax.rem(x + dx, 4) * 2 + lax.rem(y + dy, 2)


def spread(i, f):
    a, b, c = lax.rem(i, 4), lax.rem(lax.div(i, 4), 4), lax.div(i, 16)
    return step_from(f, a, lax.rem(a + b, 4), lax.rem(a + b + c, 2))


def wait_bytes(ref, sem):
    pltpu.make_async_copy(ref, ref, sem).wait()


def kernel(
    ids_ref, w_ref, tok_hbm, dout_hbm, gate_hbm, up_hbm, down_hbm,
    mq_s, droute_ref, gu_s, dn_s,
    tok_v, dout_v, code_s, wt_s, e_s, gs_s, et_s, whi_s, wlo_s, rhs_s, pm_s,
    s_s, r_s, xg_s, gu_acc, dh_acc, hid_s, dgu_s,
    xo_s, xi_s, yo_s, yi_s, v_s, sr_s, rr_s, acc_s, accq_s, dq_s, dqq_s, po_s, pi_s, dr_s,
    round_sem, tok_sem, w_sem, ssem, rsem, lsem, fs_sem, fr_sem, qs_sem, qr_sem,
    xs_sem, xr_sem, ys_sem, yr_sem, s2_sem, r2_sem, l2_sem,
    ps_sem, pr_sem, ms_sem, mr_sem, ds_sem, dr_sem,
):
    f = lax.axis_index("fsdp")
    e = lax.axis_index("expert")
    y, c = lax.div(e, 2), lax.rem(e, 2)
    mate = e + 1 - 2 * c
    other = lax.rem(e + 2, 4)

    bar = pltpu.get_barrier_semaphore()
    x_line = [(step_from(f, 0, n, 0), e) for n in (1, 3, 2)]
    z_line = [(step_from(f, n, 0, 0), e) for n in (1, 3, 2)]
    y_line = [(f, other), (step_from(f, 0, 0, 1), other), (step_from(f, 0, 0, 1), e)]

    def signal(sem, devices):
        for d in devices:
            pl.semaphore_signal(sem, inc=1, device_id=d, device_id_type=MESH)

    signal(bar, z_line + x_line + y_line + [(f, mate)])

    half = pl.ds(pl.multiple_of(c * HALF, HALF), HALF)
    tok_in = pltpu.make_async_copy(tok_hbm.at[:, half], tok_v, tok_sem.at[0])
    dout_in = pltpu.make_async_copy(dout_hbm.at[:, half], dout_v, tok_sem.at[1])
    tok_in.start()
    dout_in.start()
    for j in range(2 * NP):
        cols = pl.ds(j * W, W)
        pltpu.make_async_copy(gate_hbm.at[0, cols, :], gu_s.at[j, :, pl.ds(0, FH)], w_sem.at[0]).start()
        pltpu.make_async_copy(up_hbm.at[0, cols, :], gu_s.at[j, :, pl.ds(FH, FH)], w_sem.at[0]).start()
        pltpu.make_async_copy(down_hbm.at[0, :, cols], dn_s.at[j], w_sem.at[1]).start()

    ids = ids_ref[...]
    wts = w_ref[...]
    top = ids.shape[0]
    expert = iota((128, TOK), 0)
    named = jnp.zeros((128, TOK), F32)
    wmat_t = jnp.zeros((128, TOK), F32)
    for k in range(top):
        hit = ids[k : k + 1, :] == expert
        named = named + jnp.where(hit, 1.0, 0.0)
        wmat_t = wmat_t + jnp.where(hit, wts[k : k + 1, :], 0.0)
    earlier = jnp.where(expert < iota((128, TOK), 1), 1.0, 0.0).astype(BF)
    code_s[...] = jnp.where(named > 0.5, dot(named.astype(BF), earlier) + 1.0, 0.0)
    wt_s[...] = wmat_t

    part48, rank48 = part_and_rank(iota((MSG, TOK), 0))
    want48 = (rank48 + 1).astype(F32)

    def build_e(n, carry):
        hit = code_s[pl.ds(n, 1), :] == want48
        scale = jnp.sum(jnp.where(hit, wt_s[pl.ds(n, 1), :], 0.0), axis=1, keepdims=True)
        gs_s[n] = jnp.broadcast_to(scale, (MSG, TOK))
        for q in range(4):
            e_s[n, :, q * TOK : (q + 1) * TOK] = jnp.where(hit & (part48 == q), 1.0, 0.0).astype(BF)
        return carry

    lax.fori_loop(0, SRC, build_e, 0)

    def pack(k):
        piece = 2 + y if k == 0 else k - 1
        for q in range(4):
            cols = pl.ds(pl.multiple_of(piece * W + q * Q, Q), Q)
            rhs_s[q * TOK : (q + 1) * TOK, 0:Q] = tok_v[:, cols]
            rhs_s[q * TOK : (q + 1) * TOK, Q : 2 * Q] = dout_v[:, cols]

        def some_rows(g, carry):
            some = pl.ds(g * 4, 4)
            rows = dot(e_s[some].reshape(4 * MSG, 4 * TOK), rhs_s[...])
            cot = rows[:, Q:] * gs_s[some].reshape(4 * MSG, TOK)
            s_s[k, some, 0:MSG, :] = rows[:, :Q].astype(BF).reshape(4, MSG, Q)
            s_s[k, some, MSG : 2 * MSG, :] = cot.astype(BF).reshape(4, MSG, Q)
            return carry

        lax.fori_loop(0, SRC // 4, some_rows, 0)

    def crossed(f2):
        return lax.rem(e + 2 * lax.rem(f + f2, 2), 4)

    def send(k, f2):
        pltpu.make_async_remote_copy(
            s_s.at[k, f2], r_s.at[k, f], ssem.at[k], rsem.at[k],
            device_id=(f2, e if k == 0 else crossed(f2)), device_id_type=MESH,
        ).start()

    def send_line(k):
        def one(n, carry):
            send(k, step_from(f, n, 0, 0))
            send(k, step_from(f, 0, n, 0))
            return carry

        lax.fori_loop(1, 4, one, 0)
        send(k, step_from(f, 0, 0, 1))

    def send_plane(k):
        def one(n, carry):
            a, b = lax.div(n, 3), lax.rem(n, 3)
            send(k, step_from(f, 1 + a, 1 + lax.rem(a + b, 3), 0))
            return carry

        lax.fori_loop(0, 9, one, 0)

    def send_rest(k):
        def one(n, carry):
            a, b = lax.rem(n, 4), lax.div(n, 4)
            send(k, step_from(f, a, lax.rem(a + b, 4), 1))
            return carry

        lax.fori_loop(1, 16, one, 0)

    def keep(k):
        pltpu.make_async_copy(s_s.at[k, f], r_s.at[k, f], lsem.at[k]).start()

    tok_in.wait()
    dout_in.wait()
    pack(0)
    pl.semaphore_wait(bar, 10)
    signal(round_sem.at[0], x_line)
    send_line(0)
    pack(1)
    pl.semaphore_wait(round_sem.at[0], 3)
    signal(round_sem.at[1], y_line)
    send_plane(0)
    send_line(1)
    keep(0)
    keep(1)
    pl.semaphore_wait(round_sem.at[1], 3)
    send_rest(0)
    send_plane(1)
    send_rest(1)
    pack(2)

    def send_any(i, carry):
        send(2, spread(i, f))
        return carry

    lax.fori_loop(1, SRC, send_any, 0)
    keep(2)

    i_p = iota((4 * MSG, 4 * MSG), 0)
    q_p = over_msg(i_p)
    s_p, r_p = part_and_rank(i_p - MSG * q_p)
    pm_s[...] = jnp.where(iota((4 * MSG, 4 * MSG), 1) == MSG * s_p + CAP * q_p + r_p, 1.0, 0.0).astype(BF)
    gu_acc[...] = jnp.zeros_like(gu_acc)
    dh_acc[...] = jnp.zeros_like(dh_acc)

    wmat = wt_s[...].T
    w_hi = wmat.astype(BF)
    w_lo = (wmat - w_hi.astype(F32)).astype(BF)
    code_b = code_s[...].T.astype(BF)

    def build_et(g, carry):
        j = iota((TOK, 8 * MSG), 1)
        n = over_msg(j)
        part, rank = part_and_rank(j - MSG * n)
        rep = jnp.where(iota((TOK, 8 * MSG), 0) == n + 8 * g, 1.0, 0.0).astype(BF)
        hit = dot(code_b, rep) == (rank + 1).astype(F32)
        hi = dot(w_hi, rep)
        lo = dot(w_lo, rep)
        for q in range(4):
            here = hit & (part == q)
            rows = slice(q * TOK, (q + 1) * TOK)
            et_s[g, rows, :] = jnp.where(here, 1.0, 0.0).astype(BF)
            whi_s[g, rows, :] = jnp.where(here, hi, 0.0).astype(BF)
            wlo_s[g, rows, :] = jnp.where(here, lo, 0.0).astype(BF)
        return carry

    lax.fori_loop(0, 4, build_et, 0)
    for q in range(4):
        rows = slice(q * TOK, (q + 1) * TOK)
        for pp in range(2):
            dq_s[rows, pp * Q : (pp + 1) * Q] = dout_v[:, pp * W + q * Q : pp * W + (q + 1) * Q]
        dqq_s[rows, :] = dout_v[:, pl.ds(pl.multiple_of((2 + y) * W + q * Q, Q), Q)]
    wait_bytes(gu_s, w_sem.at[0])
    wait_bytes(dn_s, w_sem.at[1])

    def first(j):
        for n in range(3):
            cols = slice(n * 256, (n + 1) * 256)
            gu_acc[:, cols] += dot(xg_s[j, 0], gu_s[j, :, cols])
        dh_acc[...] += dot_nt(xg_s[j, 1], dn_s[j])

    order = (2 + y, 0, 1, 3 - y)

    def unpack(k):
        j = c * NP + order[k]
        wait_bytes(r_s.at[k, pl.ds(0, SRC - 1)], rsem.at[k])
        pltpu.make_async_copy(s_s.at[k, f], r_s.at[k, f], lsem.at[k]).wait()

        def some_rows(g, carry):
            some = pl.ds(g * 4, 4)
            rows = pl.ds(pl.multiple_of(g * MSG, MSG), MSG)
            x = r_s[k, some, 0:MSG, :].reshape(4 * MSG, Q)
            ct = r_s[k, some, MSG : 2 * MSG, :].reshape(4 * MSG, Q)
            out = dot(pm_s[...], jnp.concatenate([x, ct], axis=1)).astype(BF)
            for q in range(4):
                xg_s[j, 0, rows, q * Q : (q + 1) * Q] = out[q * MSG : (q + 1) * MSG, :Q]
                xg_s[j, 1, rows, q * Q : (q + 1) * Q] = out[q * MSG : (q + 1) * MSG, Q:]
            return carry

        lax.fori_loop(0, SRC // 4, some_rows, 0)

    def to_mate(k):
        j = c * NP + order[k]
        pltpu.make_async_remote_copy(
            xg_s.at[j], xg_s.at[j], fs_sem.at[k], fr_sem.at[k],
            device_id=(f, mate), device_id_type=MESH,
        ).start()

    def from_mate(k):
        j = (1 - c) * NP + order[k]
        wait_bytes(xg_s.at[j], fr_sem.at[k])
        first(j)

    unpack(0)
    here = c * NP + order[0]
    pltpu.make_async_remote_copy(
        xg_s.at[here], xg_s.at[here], qs_sem, qr_sem, device_id=(f, other), device_id_type=MESH
    ).start()
    to_mate(0)
    first(here)
    from_mate(0)
    unpack(1)
    to_mate(1)
    first(c * NP)
    from_mate(1)
    unpack(2)
    to_mate(2)
    first(c * NP + 1)
    from_mate(2)
    there = c * NP + order[3]
    wait_bytes(xg_s.at[there], qr_sem)
    to_mate(3)
    first(there)
    from_mate(3)

    def middle(n, carry):
        rows = pl.ds(pl.multiple_of(n * 96, 96), 96)
        gate = gu_acc[rows, 0:FH]
        up = gu_acc[rows, FH : 2 * FH]
        dh = dh_acc[rows, :]
        sig = jax.nn.sigmoid(gate)
        act = gate * sig
        hid_s[rows, :] = (act * up).astype(BF)
        slope = sig * (1.0 + gate * (1.0 - sig))
        dgu_s[rows, 0:FH] = (dh * up * slope).astype(BF)
        dgu_s[rows, FH : 2 * FH] = (dh * act).astype(BF)
        return carry

    lax.fori_loop(0, ROWS // 96, middle, 0)

    back = (3 - y, 0, 1, 2 + y)

    def second(a, j):
        if a == 0:
            return dot(hid_s[...], dn_s[j])
        return dot_nt(dgu_s[...], gu_s[j])

    def for_mate(a, k):
        t = 4 * a + k
        xo_s[t] = second(a, (1 - c) * NP + back[k]).astype(BF)
        pltpu.make_async_remote_copy(
            xo_s.at[t], xi_s.at[t], xs_sem.at[t], xr_sem.at[t],
            device_id=(f, mate), device_id_type=MESH,
        ).start()

    def chip_sum(a, k):
        t = 4 * a + k
        own = second(a, c * NP + back[k])
        wait_bytes(xi_s.at[t], xr_sem.at[t])
        return own + xi_s[t].astype(F32)

    def for_other(a):
        yo_s[a] = chip_sum(a, 0).astype(BF)
        pltpu.make_async_remote_copy(
            yo_s.at[a], yi_s.at[a], ys_sem.at[a], yr_sem.at[a],
            device_id=(f, other), device_id_type=MESH,
        ).start()

    def returned(a, k):
        t = 3 * a + k - 1
        total = chip_sum(a, k)
        if k == 3:
            wait_bytes(yi_s.at[a], yr_sem.at[a])
            total = total + yi_s[a].astype(F32)
        v_s[...] = total.astype(BF)

        def some_rows(g, carry):
            rows = pl.ds(pl.multiple_of(g * MSG, MSG), MSG)
            some = pl.ds(g * 4, 4)
            both = jnp.concatenate([v_s[rows, q * Q : (q + 1) * Q] for q in range(4)], axis=0)
            sr_s[t, some] = dot(pm_s[...], both).astype(BF).reshape(4, MSG, Q)
            return carry

        lax.fori_loop(0, SRC // 4, some_rows, 0)

        def send_back(i, carry):
            f2 = spread(i, f)
            pltpu.make_async_remote_copy(
                sr_s.at[t, f2], rr_s.at[t, f], s2_sem.at[t], r2_sem.at[t],
                device_id=(f2, e if k == 3 else crossed(f2)), device_id_type=MESH,
            ).start()
            return carry

        lax.fori_loop(1, SRC, send_back, 0)
        pltpu.make_async_copy(sr_s.at[t, f], rr_s.at[t, f], l2_sem.at[t]).start()

    for_mate(0, 0)
    for_mate(0, 1)
    for_other(0)
    for_mate(0, 2)
    returned(0, 1)
    for_mate(0, 3)
    returned(0, 2)
    for_mate(1, 0)
    for_mate(1, 1)
    for_other(1)
    returned(0, 3)
    for_mate(1, 2)
    returned(1, 1)
    for_mate(1, 3)
    returned(1, 2)
    returned(1, 3)

    def grads(j, carry):
        for n in range(3):
            some = slice(n * 256, (n + 1) * 256)
            gu_s[j, :, some] = dot_tn(xg_s[j, 0], dgu_s[:, some]).astype(BF)
        dn_s[j] = dot_tn(hid_s[...], xg_s[j, 1]).astype(BF)
        return carry

    lax.fori_loop(0, 2 * NP, grads, 0)

    def landed(a, k):
        t = 3 * a + k
        wait_bytes(rr_s.at[t, pl.ds(0, SRC - 1)], r2_sem.at[t])
        pltpu.make_async_copy(sr_s.at[t, f], rr_s.at[t, f], l2_sem.at[t]).wait()

    def block(t, g):
        return rr_s[t, pl.ds(g * 8, 8)].reshape(8 * MSG, Q)

    def pair(a, g):
        return jnp.concatenate([block(3 * a, g), block(3 * a + 1, g)], axis=1)

    base = c * NP

    def share_partial(a):
        for pp in range(2):
            for q in range(4):
                po_s[a, pp, :, q * Q : (q + 1) * Q] = acc_s[
                    q * TOK : (q + 1) * TOK, pp * Q : (pp + 1) * Q
                ].astype(BF)
        pltpu.make_async_remote_copy(
            po_s.at[a], pi_s.at[a], ps_sem.at[2 * a], pr_sem.at[2 * a],
            device_id=(f, other), device_id_type=MESH,
        ).start()

    def share_whole(a):
        n = base + 2 + y
        for q in range(4):
            mq_s[a, n, :, q * Q : (q + 1) * Q] = accq_s[q * TOK : (q + 1) * TOK, :].astype(BF)
        pltpu.make_async_remote_copy(
            mq_s.at[a, n], mq_s.at[a, n], ps_sem.at[2 * a + 1], pr_sem.at[2 * a + 1],
            device_id=(f, other), device_id_type=MESH,
        ).start()

    def hand_over(a, h):
        some = pl.ds(base + 2 * h, 2)
        pltpu.make_async_remote_copy(
            mq_s.at[a, some], mq_s.at[a, some], ms_sem.at[2 * a + h], mr_sem.at[2 * a + h],
            device_id=(f, mate), device_id_type=MESH,
        ).start()

    def add_partial(a):
        wait_bytes(pi_s.at[a], pr_sem.at[2 * a])
        mq_s[a, pl.ds(base, 2)] = (po_s[a].astype(F32) + pi_s[a].astype(F32)).astype(BF)
        hand_over(a, 0)

    def pass_whole(a):
        wait_bytes(mq_s.at[a, base + 3 - y], pr_sem.at[2 * a + 1])
        hand_over(a, 1)

    def complete(a):
        for h in range(2):
            wait_bytes(mq_s.at[a, pl.ds((1 - c) * NP + 2 * h, 2)], mr_sem.at[2 * a + h])

    for k in range(3):
        landed(0, k)
    acc_s[...] = jnp.zeros_like(acc_s)
    accq_s[...] = jnp.zeros_like(accq_s)
    dr_s[0] = jnp.zeros((TOK, 128), F32)

    def combine_out(g, carry):
        u, v = pair(0, g), block(2, g)
        acc_s[...] += dot(whi_s[g], u) + dot(wlo_s[g], u)
        accq_s[...] += dot(whi_s[g], v) + dot(wlo_s[g], v)
        prod = dot_nt(dq_s[...], u) + dot_nt(dqq_s[...], v)
        kept = jnp.where(et_s[g] > 0, prod, 0.0)
        total = kept[0:TOK] + kept[TOK : 2 * TOK] + kept[2 * TOK : 3 * TOK] + kept[3 * TOK :]
        hi = total.astype(BF)
        lo = (total - hi.astype(F32)).astype(BF)
        rep = jnp.where(
            iota((8 * MSG, 128), 1) == over_msg(iota((8 * MSG, 128), 0)) + 8 * g, 1.0, 0.0
        ).astype(BF)
        dr_s[0] += dot(hi, rep) + dot(lo, rep)
        return carry

    lax.fori_loop(0, 4, combine_out, 0)
    share_partial(0)
    share_whole(0)

    def sum_route(n, device):
        copy = pltpu.make_async_remote_copy(
            dr_s.at[2 * n], dr_s.at[2 * n + 1], ds_sem.at[n], dr_sem.at[n],
            device_id=(f, device), device_id_type=MESH,
        )
        copy.start()
        return copy

    route = sum_route(0, other)
    add_partial(0)
    pass_whole(0)
    route.wait()
    dr_s[2] = dr_s[0] + dr_s[1]
    route = sum_route(1, mate)
    route.wait()
    total = (dr_s[2] + dr_s[3]).T
    for k in range(top):
        hit = ids_ref[k : k + 1, :] == expert
        droute_ref[k : k + 1, :] = jnp.sum(jnp.where(hit, total, 0.0), axis=0, keepdims=True)

    landed(1, 0)
    landed(1, 1)
    acc_s[...] = jnp.zeros_like(acc_s)
    accq_s[...] = jnp.zeros_like(accq_s)

    def combine_pair(g, carry):
        acc_s[...] += dot(et_s[g], pair(1, g))
        return carry

    lax.fori_loop(0, 4, combine_pair, 0)
    share_partial(1)
    landed(1, 2)

    def combine_whole(g, carry):
        accq_s[...] += dot(et_s[g], block(5, g))
        return carry

    lax.fori_loop(0, 4, combine_whole, 0)
    share_whole(1)
    add_partial(1)
    pass_whole(1)
    complete(0)
    complete(1)

    for k in range(3):
        wait_bytes(s_s.at[k, pl.ds(0, SRC - 1)], ssem.at[k])
    wait_bytes(xg_s.at[0], qs_sem)
    for k in range(4):
        wait_bytes(xg_s.at[0], fs_sem.at[k])
    for t in range(8):
        wait_bytes(xo_s.at[t], xs_sem.at[t])
    for t in range(6):
        wait_bytes(sr_s.at[t, pl.ds(0, SRC - 1)], s2_sem.at[t])
    for a in range(2):
        wait_bytes(yo_s.at[a], ys_sem.at[a])
        wait_bytes(po_s.at[a], ps_sem.at[2 * a])
        wait_bytes(mq_s.at[a, 0], ps_sem.at[2 * a + 1])
        for h in range(2):
            wait_bytes(mq_s.at[a, pl.ds(0, 2)], ms_sem.at[2 * a + h])


def store_kernel(
    mq_ref, droute_ref, gu_ref, dn_ref,
    moe_hbm, dtok_hbm, out_ref, dgate_hbm, dup_hbm, ddown_hbm, sem,
):
    copies = []
    for j in range(2 * NP):
        cols = pl.ds(j * W, W)
        copies += [
            (gu_ref.at[j, :, pl.ds(0, FH)], dgate_hbm.at[0, cols, :]),
            (gu_ref.at[j, :, pl.ds(FH, FH)], dup_hbm.at[0, cols, :]),
            (dn_ref.at[j], ddown_hbm.at[0, :, cols]),
        ]
    for a, out_hbm in enumerate((moe_hbm, dtok_hbm)):
        for n in range(2 * NP):
            copies.append((mq_ref.at[a, n], out_hbm.at[:, pl.ds(n * W, W)]))
    copies = [pltpu.make_async_copy(s, d, sem.at[n]) for n, (s, d) in enumerate(copies)]
    for one in copies:
        one.start()
    out_ref[...] = droute_ref[...]
    for one in copies:
        one.wait()


def per_device(tokens, expert_ids, route_weights, d_out, gate_weight, up_weight, down_weight):
    hbm = pl.BlockSpec(memory_space=pl.ANY)
    vmem = pl.BlockSpec(memory_space=pltpu.VMEM)
    shape = jax.ShapeDtypeStruct
    dma = pltpu.SemaphoreType.DMA
    v = pltpu.VMEM
    top = route_weights.shape[1]
    mq, droute, gu, dn = pl.pallas_call(
        kernel,
        out_shape=(
            v((2, 2 * NP, TOK, W), BF), v((top, TOK), F32),
            v((2 * NP, W, 2 * FH), BF), v((2 * NP, FH, W), BF),
        ),
        in_specs=[vmem, vmem, hbm, hbm, hbm, hbm, hbm],
        out_specs=(vmem, vmem, vmem, vmem),
        scratch_shapes=[
            v((TOK, HALF), BF), v((TOK, HALF), BF),
            v((128, TOK), F32), v((128, TOK), F32),
            v((SRC, MSG, 4 * TOK), BF), v((SRC, MSG, TOK), F32),
            v((4, 4 * TOK, 8 * MSG), BF), v((4, 4 * TOK, 8 * MSG), BF), v((4, 4 * TOK, 8 * MSG), BF),
            v((4 * TOK, 2 * Q), BF), v((4 * MSG, 4 * MSG), BF),
            v((3, SRC, 2 * MSG, Q), BF), v((3, SRC, 2 * MSG, Q), BF),
            v((2 * NP, 2, ROWS, W), BF),
            v((ROWS, 2 * FH), F32), v((ROWS, FH), F32),
            v((ROWS, FH), BF), v((ROWS, 2 * FH), BF),
            v((8, ROWS, W), BF), v((8, ROWS, W), BF),
            v((2, ROWS, W), BF), v((2, ROWS, W), BF), v((ROWS, W), BF),
            v((6, SRC, MSG, Q), BF), v((6, SRC, MSG, Q), BF),
            v((4 * TOK, 2 * Q), F32), v((4 * TOK, Q), F32),
            v((4 * TOK, 2 * Q), BF), v((4 * TOK, Q), BF),
            v((2, 2, TOK, W), BF), v((2, 2, TOK, W), BF),
            v((4, TOK, 128), F32),
            pltpu.SemaphoreType.REGULAR((2,)),
            dma((2,)), dma((2,)), dma((3,)), dma((3,)), dma((3,)), dma((4,)), dma((4,)), dma, dma,
            dma((8,)), dma((8,)), dma((2,)), dma((2,)), dma((6,)), dma((6,)), dma((6,)),
            dma((4,)), dma((4,)), dma((4,)), dma((4,)), dma((2,)), dma((2,)),
        ],
        compiler_params=pltpu.CompilerParams(
            collective_id=0, has_side_effects=True, vmem_limit_bytes=46 * 1024 * 1024
        ),
        cost_estimate=pl.CostEstimate(flops=11_000_000_000, bytes_accessed=12_000_000, transcendentals=200_000),
    )(expert_ids.T, route_weights.T, tokens, d_out, gate_weight, up_weight, down_weight)
    moe, dtok, droute, dgate, dup, ddown = pl.pallas_call(
        store_kernel,
        out_shape=(
            shape((TOK, D), BF), shape((TOK, D), BF), shape((top, TOK), F32),
            shape(gate_weight.shape, BF), shape(up_weight.shape, BF), shape(down_weight.shape, BF),
        ),
        in_specs=[vmem, vmem, vmem, vmem],
        out_specs=(hbm, hbm, vmem, hbm, hbm, hbm),
        scratch_shapes=[dma((10 * NP,))],
        compiler_params=pltpu.CompilerParams(vmem_limit_bytes=1024 * 1024),
        cost_estimate=pl.CostEstimate(flops=0, bytes_accessed=12_000_000, transcendentals=0),
    )(mq, droute, gu, dn)
    return moe, dtok, droute.T, dgate, dup, ddown


def solution(mesh):
    in_specs = (
        P("fsdp", None),
        P("fsdp", None),
        P("fsdp", None),
        P("fsdp", None),
        P("fsdp", None, "expert"),
        P("fsdp", None, "expert"),
        P("fsdp", "expert", None),
    )
    out_specs = (
        P("fsdp", None),
        P("fsdp", None),
        P("fsdp", None),
        P("fsdp", None, "expert"),
        P("fsdp", None, "expert"),
        P("fsdp", "expert", None),
    )
    return jax.shard_map(
        per_device, mesh=mesh, in_specs=in_specs, out_specs=out_specs, check_vma=False
    )
```

time: 135 us -> 122 us (0.904)
  local copies, waits for them, and re-layouts: 16.8 us -> 0 us
  Pallas kernels: 115 us -> 119 us
    unnamed x13 -> x0, local copies, waits for them, and re-layouts: 15.1 us -> none
    pallas_call x1 -> x2, Pallas kernels: 115 us -> 119 us  [the longest x1 114 us: per_device(): pl.pallas_call(kernel, out_shape=(v((2, 2 * NP, TOK, W), BF), v((top, TOK...]
    pallas_call x1 -> x0, local copies, waits for them, and re-layouts: 1.65 us -> none  [per_device(): pl.pallas_call(kernel, out_shape=(shape((TOK, D), BF), shape((TOK, D), BF...]
where the time goes in v2:
time: 122 us; the launch traced here: 120 us
  Pallas kernels  119 us (98%)
    pallas_call x1, Pallas kernels, per_device(): pl.pallas_call(kernel, out_shape=(v((2, 2 * NP, TOK, W), BF), v((top, TOK...  114 us
    pallas_call x1, Pallas kernels, per_device(): pl.pallas_call(store_kernel, out_shape=(shape((TOK, D), BF), shape((TOK,...  5.14 us

profile of v2, /device:TPU:0, one launch (start us, length us, event | category | flops | bytes accessed | tf_op | source)
XLA Modules:
  0.0 119.7 jit_solution(15774408169383376303)
XLA Ops:
  0.6 113.9 %shard_map.118 = (bf16[2,8,128,512]{3,2,1,0:T(8,128)(2,1)S(1)}, f32[8,128]{1,0:T(8,128)S(1)}, bf16[8,512,768]{2,1,0:T(8,128)(2,1)S(1)}, bf16[8,384,512]{2,1,0:T(8,128)(2,1)S(1)}) custom-call(s32[8,128]{1,0:T(8,128)} %bitcast.3, f32[8,128]{1,0:T(8,128)} %bitcast.4, bf16[128,4096]{1,0:T(8,128)(2,1)} %tok_hbm.1, bf16[128,4096]{1,0:T(8,128)(2,1)} %dout_hbm.1, ...), custom_call_target="tpu_custom_call" | custom-call | flops 11000000512 | bytes 12000000 | tf_op jit(solution)/shard_map/pallas_call | solution.py:576
  114.6 5.1 %shard_map.119 = (bf16[128,4096]{1,0:T(8,128)(2,1)}, bf16[128,4096]{1,0:T(8,128)(2,1)}, f32[8,128]{1,0:T(8,128)}, bf16[1,4096,384]{2,1,0:T(8,128)(2,1)}, bf16[1,...) custom-call(bf16[2,8,128,512]{3,2,1,0:T(8,128)(2,1)S(1)} %get-tuple-element.16.mq_ref, ...), custom_call_target="tpu_custom_call" | custom-call | bytes 12000000 | tf_op jit(solution)/shard_map/pallas_call | solution.py:611

commit v3 on v2

v3 whole, which is shorter than its diff:
```python
import jax
import jax.numpy as jnp
from jax import lax
from jax.experimental import pallas as pl
from jax.experimental.pallas import tpu as pltpu
from jax.sharding import PartitionSpec as P

MESH = pl.DeviceIdType.MESH
BF = jnp.bfloat16
F32 = jnp.float32

D = 4096
FH = 384
SRC = 32
TOK = 128
CAP = 12
ROWS = SRC * CAP
W = 512
MSG = 4 * CAP
Q = W // 4
HALF = D // 2
NP = HALF // W


def dot(a, b):
    return lax.dot_general(a, b, (((1,), (0,)), ((), ())), preferred_element_type=F32)


def dot_nt(a, b):
    return lax.dot_general(a, b, (((1,), (1,)), ((), ())), preferred_element_type=F32)


def dot_tn(a, b):
    return lax.dot_general(a, b, (((0,), (0,)), ((), ())), preferred_element_type=F32)


def iota(shape, dim):
    return lax.broadcasted_iota(jnp.int32, shape, dim)


def over_cap(j):
    return (j * 5462) >> 16


def to_message(rows, s):
    some = slice(s * CAP, (s + 1) * CAP)
    return jnp.concatenate([rows[some, q * Q : (q + 1) * Q] for q in range(4)], axis=0)


def from_messages(msgs, q):
    return jnp.concatenate([msgs[s, q * CAP : (q + 1) * CAP, :] for s in range(4)], axis=0)


def step_from(f, dz, dx, dy):
    z, x, y = lax.div(f, 8), lax.rem(lax.div(f, 2), 4), lax.rem(f, 2)
    return lax.rem(z + dz, 4) * 8 + lax.rem(x + dx, 4) * 2 + lax.rem(y + dy, 2)


def spread(i, f):
    a, b, c = lax.rem(i, 4), lax.rem(lax.div(i, 4), 4), lax.div(i, 16)
    return step_from(f, a, lax.rem(a + b, 4), lax.rem(a + b + c, 2))


def wait_bytes(ref, sem):
    pltpu.make_async_copy(ref, ref, sem).wait()


def kernel(
    ids_hbm, w_hbm, tok_hbm, dout_hbm, gate_hbm, up_hbm, down_hbm,
    mq_s, droute_ref, gu_s, dn_s,
    ids_s, w_s, tok_v, dout_v, e_s, gs_s, et_s, whi_s, wlo_s, t_s,
    sq_s, rq_s, sb_s, rb_s, xg_s, gu_acc, dh_acc, hid_s, dgu_s,
    xo_s, xi_s, yo_s, yi_s, v_s, vq_s, sr_s, rr_s, u_s, po_s, pi_s, dr_s,
    round_sem, tok_sem, w_sem, ssem, rsem, lsem, fs_sem, fr_sem, qs_sem, qr_sem,
    xs_sem, xr_sem, ys_sem, yr_sem, s2_sem, r2_sem, l2_sem,
    ps_sem, pr_sem, ms_sem, mr_sem, ds_sem, dr_sem,
):
    f = lax.axis_index("fsdp")
    e = lax.axis_index("expert")
    y, c = lax.div(e, 2), lax.rem(e, 2)
    mate = e + 1 - 2 * c
    other = lax.rem(e + 2, 4)

    bar = pltpu.get_barrier_semaphore()
    x_line = [(step_from(f, 0, n, 0), e) for n in (1, 3, 2)]
    z_line = [(step_from(f, n, 0, 0), e) for n in (1, 3, 2)]
    y_line = [(f, other), (step_from(f, 0, 0, 1), other), (step_from(f, 0, 0, 1), e)]

    def signal(sem, devices):
        for d in devices:
            pl.semaphore_signal(sem, inc=1, device_id=d, device_id_type=MESH)

    signal(bar, z_line + x_line + y_line + [(f, mate)])

    ids_in = pltpu.make_async_copy(ids_hbm, ids_s, tok_sem.at[2])
    w_in = pltpu.make_async_copy(w_hbm, w_s, tok_sem.at[3])
    ids_in.start()
    w_in.start()
    half = pl.ds(pl.multiple_of(c * HALF, HALF), HALF)
    tok_in = pltpu.make_async_copy(tok_hbm.at[:, half], tok_v, tok_sem.at[0])
    dout_in = pltpu.make_async_copy(dout_hbm.at[:, half], dout_v, tok_sem.at[1])
    tok_in.start()
    dout_in.start()

    ids_in.wait()
    w_in.wait()
    top = ids_s.shape[0]
    expert = iota((128, TOK), 0)
    named = jnp.zeros((128, TOK), F32)
    wmat = jnp.zeros((128, TOK), F32)
    for k in range(top):
        hit = ids_s[k : k + 1, :] == expert
        named = named + jnp.where(hit, 1.0, 0.0)
        wmat = wmat + jnp.where(hit, w_s[k : k + 1, :], 0.0)
    earlier = jnp.where(expert < iota((128, TOK), 1), 1.0, 0.0).astype(BF)
    code = jnp.where(named > 0.5, dot(named.astype(BF), earlier) + 1.0, 0.0)
    w_hi = wmat.astype(BF)
    w_mid = (wmat - w_hi.astype(F32)).astype(BF)
    w_lo = (wmat - w_hi.astype(F32) - w_mid.astype(F32)).astype(BF)

    slot = iota((ROWS, 128), 0)
    owner = over_cap(slot)
    rep = jnp.where(owner == iota((ROWS, 128), 1), 1.0, 0.0).astype(BF)
    fills = dot(rep, code.astype(BF)) == (slot - CAP * owner + 1).astype(F32)
    e_s[...] = jnp.where(fills, 1.0, 0.0).astype(BF)
    scale = (dot(rep, w_hi) + dot(rep, w_mid)) + dot(rep, w_lo)
    scale = jnp.sum(jnp.where(fills, scale, 0.0), axis=1, keepdims=True)
    gs_s[...] = jnp.broadcast_to(scale, (ROWS, 128))

    def rows_of(h, piece, at):
        for n in range(2):
            cols = pl.ds(pl.multiple_of(piece * W + n * 256, 256), 256)
            here = at * W + n * 256
            if h == 0:
                t_s[:, here : here + 256] = dot(e_s[...], tok_v[:, cols])
            else:
                cot = dot(e_s[...], dout_v[:, cols])
                for m in range(2):
                    t_s[:, here + m * Q : here + (m + 1) * Q] = cot[:, m * Q : (m + 1) * Q] * gs_s[...]

    def pack_one(h):
        for at in range(2):
            rows_of(h, 2 + lax.rem(y + f + at, 2), at)

        def some_rows(g, carry):
            rows = pl.ds(pl.multiple_of(g * MSG, MSG), MSG)
            for s in range(4):
                some = t_s[rows, (s % 2) * W : (s % 2 + 1) * W]
                sq_s[h, g * 4 + s] = to_message(some, s).astype(BF)
            return carry

        lax.fori_loop(0, SRC // 4, some_rows, 0)

    def pack_two(h):
        for at in range(2):
            rows_of(h, at, at)

        def some_rows(g, carry):
            rows = pl.ds(pl.multiple_of(g * MSG, MSG), MSG)
            for at in range(2):
                some = t_s[rows, at * W : (at + 1) * W]
                for s in range(4):
                    sb_s[h, g * 4 + s, at * MSG : (at + 1) * MSG, :] = to_message(some, s).astype(BF)
            return carry

        lax.fori_loop(0, SRC // 4, some_rows, 0)

    def crossed(f2):
        return lax.rem(e + 2 * lax.rem(f + f2, 2), 4)

    def send_one(h, f2):
        pltpu.make_async_remote_copy(
            sq_s.at[h, f2], rq_s.at[h, f], ssem.at[h], rsem.at[h],
            device_id=(f2, crossed(f2)), device_id_type=MESH,
        ).start()

    def send_two(h, f2):
        pltpu.make_async_remote_copy(
            sb_s.at[h, f2], rb_s.at[h, f], ssem.at[2 + h], rsem.at[2 + h],
            device_id=(f2, crossed(f2)), device_id_type=MESH,
        ).start()

    def to_line(send):
        def one(n, carry):
            send(0, step_from(f, n, 0, 0))
            send(0, step_from(f, 0, n, 0))
            return carry

        lax.fori_loop(1, 4, one, 0)
        send(0, step_from(f, 0, 0, 1))

    def to_plane(send):
        def one(n, carry):
            a, b = lax.div(n, 3), lax.rem(n, 3)
            send(0, step_from(f, 1 + a, 1 + lax.rem(a + b, 3), 0))
            return carry

        lax.fori_loop(0, 9, one, 0)

    def to_rest(send):
        def one(n, carry):
            a, b = lax.rem(n, 4), lax.div(n, 4)
            send(0, step_from(f, a, lax.rem(a + b, 4), 1))
            return carry

        lax.fori_loop(1, 16, one, 0)

    def to_all(send, h):
        def one(n, carry):
            send(h, spread(n, f))
            return carry

        lax.fori_loop(1, SRC, one, 0)

    tok_in.wait()
    pack_one(0)
    pl.semaphore_wait(bar, 10)
    signal(round_sem.at[0], x_line)
    to_line(send_one)
    pack_two(0)
    pl.semaphore_wait(round_sem.at[0], 3)
    signal(round_sem.at[1], y_line)
    to_plane(send_one)
    to_line(send_two)
    dout_in.wait()
    pack_one(1)
    pl.semaphore_wait(round_sem.at[1], 3)
    to_rest(send_one)
    to_plane(send_two)
    to_rest(send_two)
    to_all(send_one, 1)
    pack_two(1)
    to_all(send_two, 1)
    for h in range(2):
        pltpu.make_async_copy(sq_s.at[h, f], rq_s.at[h, f], lsem.at[h]).start()
        pltpu.make_async_copy(sb_s.at[h, f], rb_s.at[h, f], lsem.at[2 + h]).start()
    for j in range(2 * NP):
        cols = pl.ds(j * W, W)
        pltpu.make_async_copy(gate_hbm.at[0, cols, :], gu_s.at[j, :, pl.ds(0, FH)], w_sem.at[0]).start()
        pltpu.make_async_copy(up_hbm.at[0, cols, :], gu_s.at[j, :, pl.ds(FH, FH)], w_sem.at[0]).start()
        pltpu.make_async_copy(down_hbm.at[0, :, cols], dn_s.at[j], w_sem.at[1]).start()

    gu_acc[...] = jnp.zeros_like(gu_acc)
    dh_acc[...] = jnp.zeros_like(dh_acc)
    slot_t = iota((TOK, ROWS), 1)
    owner_t = over_cap(slot_t)
    rep_t = jnp.where(owner_t == iota((TOK, ROWS), 0), 1.0, 0.0).astype(BF)
    fills_t = dot(code.T.astype(BF), rep_t) == (slot_t - CAP * owner_t + 1).astype(F32)
    et_s[...] = jnp.where(fills_t, 1.0, 0.0).astype(BF)
    wmat_t = wmat.T
    w_hi_t = wmat_t.astype(BF)
    w_lo_t = (wmat_t - w_hi_t.astype(F32)).astype(BF)
    whi_s[...] = jnp.where(fills_t, dot(w_hi_t, rep_t), 0.0).astype(BF)
    wlo_s[...] = jnp.where(fills_t, dot(w_lo_t, rep_t), 0.0).astype(BF)
    wait_bytes(gu_s, w_sem.at[0])
    wait_bytes(dn_s, w_sem.at[1])

    def first(h, j):
        if h == 1:
            dh_acc[...] += dot_nt(xg_s[j, 1], dn_s[j])
            return
        for n in range(3):
            cols = slice(n * 256, (n + 1) * 256)
            gu_acc[:, cols] += dot(xg_s[j, 0], gu_s[j, :, cols])

    order = (2 + y, 0, 1, 3 - y)
    base = c * NP
    far = (1 - c) * NP

    def unpack(h, msgs, n, pieces):
        wait_bytes(msgs.at[h, pl.ds(0, SRC - 1)], rsem.at[2 * n + h])
        sent = (sq_s, sb_s)[n]
        pltpu.make_async_copy(sent.at[h, f], msgs.at[h, f], lsem.at[2 * n + h]).wait()

        def some_rows(g, carry):
            rows = pl.ds(pl.multiple_of(g * MSG, MSG), MSG)
            some = msgs[h, pl.ds(g * 4, 4)].astype(F32)
            for at, piece in enumerate(pieces):
                part = some[:, at * MSG : (at + 1) * MSG, :]
                for q in range(4):
                    xg_s[base + piece, h, rows, q * Q : (q + 1) * Q] = from_messages(part, q).astype(BF)
            return carry

        lax.fori_loop(0, SRC // 4, some_rows, 0)

    def to_mate(h, k):
        j = base + order[k]
        pltpu.make_async_remote_copy(
            xg_s.at[j, h], xg_s.at[j, h], fs_sem.at[4 * h + k], fr_sem.at[4 * h + k],
            device_id=(f, mate), device_id_type=MESH,
        ).start()

    def from_mate(h, k):
        j = far + order[k]
        wait_bytes(xg_s.at[j, h], fr_sem.at[4 * h + k])
        first(h, j)

    def get_one(h):
        j = base + order[0]
        unpack(h, rq_s, 0, order[0:1])
        pltpu.make_async_remote_copy(
            xg_s.at[j, h], xg_s.at[j, h], qs_sem.at[h], qr_sem.at[h],
            device_id=(f, other), device_id_type=MESH,
        ).start()
        to_mate(h, 0)

    def get_rest(h):
        first(h, base + order[0])
        from_mate(h, 0)
        unpack(h, rb_s, 1, order[1:3])
        to_mate(h, 1)
        to_mate(h, 2)
        first(h, base + order[1])
        first(h, base + order[2])
        there = base + order[3]
        wait_bytes(xg_s.at[there, h], qr_sem.at[h])
        to_mate(h, 3)
        first(h, there)
        for k in range(1, 4):
            from_mate(h, k)

    def middle(h):
        def some_rows(n, carry):
            rows = pl.ds(pl.multiple_of(n * 96, 96), 96)
            gate = gu_acc[rows, 0:FH]
            up = gu_acc[rows, FH : 2 * FH]
            sig = jax.nn.sigmoid(gate)
            act = gate * sig
            if h == 0:
                hid_s[rows, :] = (act * up).astype(BF)
                return carry
            dh = dh_acc[rows, :]
            slope = sig * (1.0 + gate * (1.0 - sig))
            dgu_s[rows, 0:FH] = (dh * up * slope).astype(BF)
            dgu_s[rows, FH : 2 * FH] = (dh * act).astype(BF)
            return carry

        lax.fori_loop(0, ROWS // 96, some_rows, 0)

    back = ((0, 1, 2, 3), (3 - y, 0, 1, 2 + y))

    def second(a, j):
        if a == 0:
            return dot(hid_s[...], dn_s[j])
        return dot_nt(dgu_s[...], gu_s[j])

    def for_mate(a, k):
        t = 4 * a + k
        xo_s[t] = second(a, far + back[a][k]).astype(BF)
        pltpu.make_async_remote_copy(
            xo_s.at[t], xi_s.at[t], xs_sem.at[t], xr_sem.at[t],
            device_id=(f, mate), device_id_type=MESH,
        ).start()

    def chip_sum(a, k):
        t = 4 * a + k
        own = second(a, base + back[a][k])
        wait_bytes(xi_s.at[t], xr_sem.at[t])
        return own + xi_s[t].astype(F32)

    def send_back(t):
        def some_rows(g, carry):
            some = v_s[pl.ds(pl.multiple_of(g * MSG, MSG), MSG), :]
            for s in range(4):
                sr_s[t, g * 4 + s] = to_message(some, s).astype(BF)
            return carry

        lax.fori_loop(0, SRC // 4, some_rows, 0)

        def one(i, carry):
            f2 = spread(i, f)
            pltpu.make_async_remote_copy(
                sr_s.at[t, f2], rr_s.at[t, f], s2_sem.at[t], r2_sem.at[t],
                device_id=(f2, crossed(f2)), device_id_type=MESH,
            ).start()
            return carry

        lax.fori_loop(1, SRC, one, 0)
        pltpu.make_async_copy(sr_s.at[t, f], rr_s.at[t, f], l2_sem.at[t]).start()

    def returned(a, k):
        v_s[...] = chip_sum(a, k)
        send_back(3 * a + k)

    def for_other():
        same = lax.rem(over_cap(iota((ROWS, W), 0)) + f, 2) == 0
        a, b = chip_sum(1, 0), chip_sum(1, 3)
        yo_s[...] = jnp.where(same, a, b).astype(BF)
        vq_s[...] = jnp.where(same, b, a)
        pltpu.make_async_remote_copy(
            yo_s, yi_s, ys_sem, yr_sem, device_id=(f, other), device_id_type=MESH
        ).start()

    def both_chips():
        wait_bytes(yi_s, yr_sem)
        v_s[...] = vq_s[...] + yi_s[...].astype(F32)
        send_back(6)

    def grads(j, carry):
        for n in range(3):
            some = slice(n * 256, (n + 1) * 256)
            gu_s[j, :, some] = dot_tn(xg_s[j, 0], dgu_s[:, some]).astype(BF)
        dn_s[j] = dot_tn(hid_s[...], xg_s[j, 1]).astype(BF)
        return carry

    def landed(t):
        wait_bytes(rr_s.at[t, pl.ds(0, SRC - 1)], r2_sem.at[t])
        pltpu.make_async_copy(sr_s.at[t, f], rr_s.at[t, f], l2_sem.at[t]).wait()

        def some_rows(g, carry):
            rows = pl.ds(pl.multiple_of(g * MSG, MSG), MSG)
            msgs = rr_s[t, pl.ds(g * 4, 4)].astype(F32)
            for q in range(4):
                u_s[t, rows, q * Q : (q + 1) * Q] = from_messages(msgs, q).astype(BF)
            return carry

        lax.fori_loop(0, SRC // 4, some_rows, 0)

    def combined(t):
        u = u_s[t]
        if t >= 4:
            return dot(et_s[...], u).astype(BF)
        return (dot(whi_s[...], u) + dot(wlo_s[...], u)).astype(BF)

    def share_partial(n):
        for k in range(2):
            landed(2 * n + k)
            po_s[n, k] = combined(2 * n + k)
        pltpu.make_async_remote_copy(
            po_s.at[n], pi_s.at[n], ps_sem.at[n], pr_sem.at[n],
            device_id=(f, other), device_id_type=MESH,
        ).start()

    def share_whole():
        n = base + 2 + y
        landed(6)
        mq_s[1, n] = combined(6)
        pltpu.make_async_remote_copy(
            mq_s.at[1, n], mq_s.at[1, n], ps_sem.at[3], pr_sem.at[3],
            device_id=(f, other), device_id_type=MESH,
        ).start()

    def hand_over(n):
        some = pl.ds(base + 2 * (n % 2), 2)
        pltpu.make_async_remote_copy(
            mq_s.at[n // 2, some], mq_s.at[n // 2, some], ms_sem.at[n], mr_sem.at[n],
            device_id=(f, mate), device_id_type=MESH,
        ).start()

    def add_partial(n):
        wait_bytes(pi_s.at[n], pr_sem.at[n])
        some = pl.ds(base + 2 * (n % 2), 2)
        mq_s[n // 2, some] = (po_s[n].astype(F32) + pi_s[n].astype(F32)).astype(BF)
        hand_over(n)

    def pass_whole():
        wait_bytes(mq_s.at[1, base + 3 - y], pr_sem.at[3])
        hand_over(3)

    def sum_route(n, device):
        copy = pltpu.make_async_remote_copy(
            dr_s.at[2 * n], dr_s.at[2 * n + 1], ds_sem.at[n], dr_sem.at[n],
            device_id=(f, device), device_id_type=MESH,
        )
        copy.start()
        return copy

    get_one(0)
    get_rest(0)
    middle(0)
    for k in range(4):
        for_mate(0, k)
    get_one(1)
    for k in range(4):
        returned(0, k)
    get_rest(1)
    middle(1)
    for k in range(4):
        for_mate(1, k)
    for_other()
    returned(1, 1)
    returned(1, 2)
    share_partial(0)
    prod = dot_nt(dout_v[:, 0:W], u_s[0]) + dot_nt(dout_v[:, W : 2 * W], u_s[1])
    lax.fori_loop(0, NP, grads, 0)
    both_chips()
    share_partial(1)
    prod = prod + dot_nt(dout_v[:, 2 * W : 3 * W], u_s[2]) + dot_nt(dout_v[:, 3 * W :], u_s[3])
    kept = jnp.where(et_s[...] > 0, prod, 0.0)
    hi = kept.astype(BF)
    lo = (kept - hi.astype(F32)).astype(BF)
    group = jnp.where(over_cap(iota((ROWS, 128), 0)) == iota((ROWS, 128), 1), 1.0, 0.0).astype(BF)
    dr_s[0] = dot(hi, group) + dot(lo, group)
    route = sum_route(0, other)
    add_partial(0)
    lax.fori_loop(NP, 2 * NP, grads, 0)
    share_partial(2)
    add_partial(1)
    route.wait()
    dr_s[2] = dr_s[0] + dr_s[1]
    route = sum_route(1, mate)
    share_whole()
    add_partial(2)
    route.wait()
    total = (dr_s[2] + dr_s[3]).T
    for k in range(top):
        hit = ids_s[k : k + 1, :] == expert
        droute_ref[k : k + 1, :] = jnp.sum(jnp.where(hit, total, 0.0), axis=0, keepdims=True)
    pass_whole()
    for n in range(4):
        wait_bytes(mq_s.at[n // 2, pl.ds(far + 2 * (n % 2), 2)], mr_sem.at[n])

    for h in range(2):
        wait_bytes(sq_s.at[h, pl.ds(0, SRC - 1)], ssem.at[h])
        wait_bytes(sb_s.at[h, pl.ds(0, SRC - 1)], ssem.at[2 + h])
        wait_bytes(xg_s.at[0, 0], qs_sem.at[h])
    for n in range(8):
        wait_bytes(xg_s.at[0, 0], fs_sem.at[n])
        wait_bytes(xo_s.at[n], xs_sem.at[n])
    for t in range(7):
        wait_bytes(sr_s.at[t, pl.ds(0, SRC - 1)], s2_sem.at[t])
    wait_bytes(yo_s, ys_sem)
    for n in range(3):
        wait_bytes(po_s.at[n], ps_sem.at[n])
    wait_bytes(mq_s.at[1, 0], ps_sem.at[3])
    for n in range(4):
        wait_bytes(mq_s.at[n // 2, pl.ds(0, 2)], ms_sem.at[n])


def store_kernel(
    mq_ref, droute_ref, gu_ref, dn_ref,
    moe_hbm, dtok_hbm, out_ref, dgate_hbm, dup_hbm, ddown_hbm, sem,
):
    copies = []
    for j in range(2 * NP):
        cols = pl.ds(j * W, W)
        copies += [
            (gu_ref.at[j, :, pl.ds(0, FH)], dgate_hbm.at[0, cols, :]),
            (gu_ref.at[j, :, pl.ds(FH, FH)], dup_hbm.at[0, cols, :]),
            (dn_ref.at[j], ddown_hbm.at[0, :, cols]),
        ]
    for a, out_hbm in enumerate((moe_hbm, dtok_hbm)):
        for n in range(2 * NP):
            copies.append((mq_ref.at[a, n], out_hbm.at[:, pl.ds(n * W, W)]))
    copies = [pltpu.make_async_copy(s, d, sem.at[n]) for n, (s, d) in enumerate(copies)]
    for one in copies:
        one.start()
    out_ref[...] = droute_ref[...]
    for one in copies:
        one.wait()


def per_device(tokens, expert_ids, route_weights, d_out, gate_weight, up_weight, down_weight):
    hbm = pl.BlockSpec(memory_space=pl.ANY)
    vmem = pl.BlockSpec(memory_space=pltpu.VMEM)
    shape = jax.ShapeDtypeStruct
    dma = pltpu.SemaphoreType.DMA
    v = pltpu.VMEM
    top = route_weights.shape[1]
    mq, droute, gu, dn = pl.pallas_call(
        kernel,
        out_shape=(
            v((2, 2 * NP, TOK, W), BF), v((top, TOK), F32),
            v((2 * NP, W, 2 * FH), BF), v((2 * NP, FH, W), BF),
        ),
        in_specs=[hbm] * 7,
        out_specs=(vmem, vmem, vmem, vmem),
        scratch_shapes=[
            v((top, TOK), jnp.int32), v((top, TOK), F32),
            v((TOK, HALF), BF), v((TOK, HALF), BF),
            v((ROWS, TOK), BF), v((ROWS, 128), F32),
            v((TOK, ROWS), BF), v((TOK, ROWS), BF), v((TOK, ROWS), BF),
            v((ROWS, 2 * W), F32),
            v((2, SRC, MSG, Q), BF), v((2, SRC, MSG, Q), BF),
            v((2, SRC, 2 * MSG, Q), BF), v((2, SRC, 2 * MSG, Q), BF),
            v((2 * NP, 2, ROWS, W), BF),
            v((ROWS, 2 * FH), F32), v((ROWS, FH), F32),
            v((ROWS, FH), BF), v((ROWS, 2 * FH), BF),
            v((8, ROWS, W), BF), v((8, ROWS, W), BF),
            v((ROWS, W), BF), v((ROWS, W), BF), v((ROWS, W), F32), v((ROWS, W), F32),
            v((7, SRC, MSG, Q), BF), v((7, SRC, MSG, Q), BF),
            v((7, ROWS, W), BF),
            v((3, 2, TOK, W), BF), v((3, 2, TOK, W), BF),
            v((4, TOK, 128), F32),
            pltpu.SemaphoreType.REGULAR((2,)),
            dma((4,)), dma((2,)), dma((4,)), dma((4,)), dma((4,)), dma((8,)), dma((8,)), dma((2,)), dma((2,)),
            dma((8,)), dma((8,)), dma, dma, dma((7,)), dma((7,)), dma((7,)),
            dma((4,)), dma((4,)), dma((4,)), dma((4,)), dma((2,)), dma((2,)),
        ],
        compiler_params=pltpu.CompilerParams(
            collective_id=0, has_side_effects=True, vmem_limit_bytes=46 * 1024 * 1024
        ),
        cost_estimate=pl.CostEstimate(flops=11_000_000_000, bytes_accessed=12_000_000, transcendentals=200_000),
    )(expert_ids.T, route_weights.T, tokens, d_out, gate_weight, up_weight, down_weight)
    moe, dtok, droute, dgate, dup, ddown = pl.pallas_call(
        store_kernel,
        out_shape=(
            shape((TOK, D), BF), shape((TOK, D), BF), shape((top, TOK), F32),
            shape(gate_weight.shape, BF), shape(up_weight.shape, BF), shape(down_weight.shape, BF),
        ),
        in_specs=[vmem, vmem, vmem, vmem],
        out_specs=(hbm, hbm, vmem, hbm, hbm, hbm),
        scratch_shapes=[dma((10 * NP,))],
        compiler_params=pltpu.CompilerParams(vmem_limit_bytes=1024 * 1024),
        cost_estimate=pl.CostEstimate(flops=0, bytes_accessed=12_000_000, transcendentals=0),
    )(mq, droute, gu, dn)
    return moe, dtok, droute.T, dgate, dup, ddown


def solution(mesh):
    in_specs = (
        P("fsdp", None),
        P("fsdp", None),
        P("fsdp", None),
        P("fsdp", None),
        P("fsdp", None, "expert"),
        P("fsdp", None, "expert"),
        P("fsdp", "expert", None),
    )
    out_specs = (
        P("fsdp", None),
        P("fsdp", None),
        P("fsdp", None),
        P("fsdp", None, "expert"),
        P("fsdp", None, "expert"),
        P("fsdp", "expert", None),
    )
    return jax.shard_map(
        per_device, mesh=mesh, in_specs=in_specs, out_specs=out_specs, check_vma=False
    )
```

time: 122 us -> 94.2 us (0.77)
  the two profiles are of different devices: /device:TPU:0 before, /device:TPU:31 now
where the time goes in v3:
time: 94.2 us; the launch traced here: 94.1 us
  Pallas kernels  93.4 us (99%)
    pallas_call x1, Pallas kernels, per_device(): pl.pallas_call(kernel, out_shape=(v((2, 2 * NP, TOK, W), BF), v((top, TOK...  88.3 us
    pallas_call x1, Pallas kernels, per_device(): pl.pallas_call(store_kernel, out_shape=(shape((TOK, D), BF), shape((TOK,...  5.14 us

profile of v3, /device:TPU:31, one launch (start us, length us, event | category | flops | bytes accessed | tf_op | source)
XLA Modules:
  0.0 94.1 jit_solution(11632209712062639152)
XLA Ops:
  0.6 88.3 %shard_map.118 = (bf16[2,8,128,512]{3,2,1,0:T(8,128)(2,1)S(1)}, f32[8,128]{1,0:T(8,128)S(1)}, bf16[8,512,768]{2,1,0:T(8,128)(2,1)S(1)}, bf16[8,384,512]{2,1,0:T(8,128)(2,1)S(1)}) custom-call(s32[8,128]{1,0:T(8,128)} %bitcast.3, f32[8,128]{1,0:T(8,128)} %bitcast.4, bf16[128,4096]{1,0:T(8,128)(2,1)} %tok_hbm.1, bf16[128,4096]{1,0:T(8,128)(2,1)} %dout_hbm.1, ...), custom_call_target="tpu_custom_call" | custom-call | flops 11000000512 | bytes 12000000 | tf_op jit(solution)/shard_map/pallas_call | solution.py:560
  88.9 5.1 %shard_map.119 = (bf16[128,4096]{1,0:T(8,128)(2,1)}, bf16[128,4096]{1,0:T(8,128)(2,1)}, f32[8,128]{1,0:T(8,128)}, bf16[1,4096,384]{2,1,0:T(8,128)(2,1)}, bf16[1,...) custom-call(bf16[2,8,128,512]{3,2,1,0:T(8,128)(2,1)S(1)} %get-tuple-element.16.mq_ref, ...), custom_call_target="tpu_custom_call" | custom-call | bytes 12000000 | tf_op jit(solution)/shard_map/pallas_call | solution.py:595

commit v4 on v3

--- a/solution.py
+++ b/solution.py
@@ -180,27 +180,27 @@
             device_id=(f2, crossed(f2)), device_id_type=MESH,
         ).start()
 
-    def to_line(send):
+    def to_line(send, h):
         def one(n, carry):
-            send(0, step_from(f, n, 0, 0))
-            send(0, step_from(f, 0, n, 0))
+            send(h, step_from(f, n, 0, 0))
+            send(h, step_from(f, 0, n, 0))
             return carry
 
         lax.fori_loop(1, 4, one, 0)
-        send(0, step_from(f, 0, 0, 1))
-
-    def to_plane(send):
+        send(h, step_from(f, 0, 0, 1))
+
+    def to_plane(send, h):
         def one(n, carry):
             a, b = lax.div(n, 3), lax.rem(n, 3)
-            send(0, step_from(f, 1 + a, 1 + lax.rem(a + b, 3), 0))
+            send(h, step_from(f, 1 + a, 1 + lax.rem(a + b, 3), 0))
             return carry
 
         lax.fori_loop(0, 9, one, 0)
 
-    def to_rest(send):
+    def to_rest(send, h):
         def one(n, carry):
             a, b = lax.rem(n, 4), lax.div(n, 4)
-            send(0, step_from(f, a, lax.rem(a + b, 4), 1))
+            send(h, step_from(f, a, lax.rem(a + b, 4), 1))
             return carry
 
         lax.fori_loop(1, 16, one, 0)
@@ -211,34 +211,263 @@
             return carry
 
         lax.fori_loop(1, SRC, one, 0)
+
+    def one_sent(h):
+        wait_bytes(sq_s.at[h, pl.ds(0, SRC - 1)], ssem.at[h])
+
+    def two_sent(h):
+        wait_bytes(sb_s.at[h, pl.ds(0, SRC - 1)], ssem.at[2 + h])
+
+    def keep(h):
+        pltpu.make_async_copy(sq_s.at[h, f], rq_s.at[h, f], lsem.at[h]).start()
+
+    def keep_two(h):
+        pltpu.make_async_copy(sb_s.at[h, f], rb_s.at[h, f], lsem.at[2 + h]).start()
 
     tok_in.wait()
     pack_one(0)
     pl.semaphore_wait(bar, 10)
     signal(round_sem.at[0], x_line)
-    to_line(send_one)
-    pack_two(0)
+    to_line(send_one, 0)
+    dout_in.wait()
+    pack_one(1)
     pl.semaphore_wait(round_sem.at[0], 3)
     signal(round_sem.at[1], y_line)
-    to_plane(send_one)
-    to_line(send_two)
-    dout_in.wait()
-    pack_one(1)
+    to_plane(send_one, 0)
+    to_line(send_one, 1)
+    pack_two(0)
     pl.semaphore_wait(round_sem.at[1], 3)
-    to_rest(send_one)
-    to_plane(send_two)
-    to_rest(send_two)
-    to_all(send_one, 1)
-    pack_two(1)
-    to_all(send_two, 1)
-    for h in range(2):
-        pltpu.make_async_copy(sq_s.at[h, f], rq_s.at[h, f], lsem.at[h]).start()
-        pltpu.make_async_copy(sb_s.at[h, f], rb_s.at[h, f], lsem.at[2 + h]).start()
+    to_rest(send_one, 0)
+    to_plane(send_one, 1)
+    keep(0)
+    one_sent(0)
+    to_rest(send_one, 1)
+    keep(1)
+    one_sent(1)
+    to_all(send_two, 0)
     for j in range(2 * NP):
         cols = pl.ds(j * W, W)
         pltpu.make_async_copy(gate_hbm.at[0, cols, :], gu_s.at[j, :, pl.ds(0, FH)], w_sem.at[0]).start()
         pltpu.make_async_copy(up_hbm.at[0, cols, :], gu_s.at[j, :, pl.ds(FH, FH)], w_sem.at[0]).start()
         pltpu.make_async_copy(down_hbm.at[0, :, cols], dn_s.at[j], w_sem.at[1]).start()
+
+    def first(h, j):
+        if h == 1:
+            dh_acc[...] += dot_nt(xg_s[j, 1], dn_s[j])
+            return
+        for n in range(3):
+            cols = slice(n * 256, (n + 1) * 256)
+            gu_acc[:, cols] += dot(xg_s[j, 0], gu_s[j, :, cols])
+
+    order = (2 + y, 0, 1, 3 - y)
+    base = c * NP
+    far = (1 - c) * NP
+
+    def unpack(h, msgs, n, pieces):
+        wait_bytes(msgs.at[h, pl.ds(0, SRC - 1)], rsem.at[2 * n + h])
+        sent = (sq_s, sb_s)[n]
+        pltpu.make_async_copy(sent.at[h, f], msgs.at[h, f], lsem.at[2 * n + h]).wait()
+
+        def some_rows(g, carry):
+            rows = pl.ds(pl.multiple_of(g * MSG, MSG), MSG)
+            some = msgs[h, pl.ds(g * 4, 4)].astype(F32)
+            for at, piece in enumerate(pieces):
+                part = some[:, at * MSG : (at + 1) * MSG, :]
+                for q in range(4):
+                    xg_s[base + piece, h, rows, q * Q : (q + 1) * Q] = from_messages(part, q).astype(BF)
+            return carry
+
+        lax.fori_loop(0, SRC // 4, some_rows, 0)
+
+    def to_mate(h, k):
+        j = base + order[k]
+        pltpu.make_async_remote_copy(
+            xg_s.at[j, h], xg_s.at[j, h], fs_sem.at[4 * h + k], fr_sem.at[4 * h + k],
+            device_id=(f, mate), device_id_type=MESH,
+        ).start()
+
+    def from_mate(h, k):
+        j = far + order[k]
+        wait_bytes(xg_s.at[j, h], fr_sem.at[4 * h + k])
+        first(h, j)
+
+    def get_one(h):
+        j = base + order[0]
+        unpack(h, rq_s, 0, order[0:1])
+        pltpu.make_async_remote_copy(
+            xg_s.at[j, h], xg_s.at[j, h], qs_sem.at[h], qr_sem.at[h],
+            device_id=(f, other), device_id_type=MESH,
+        ).start()
+        to_mate(h, 0)
+
+    def use_one(h):
+        first(h, base + order[0])
+        from_mate(h, 0)
+
+    def get_rest(h):
+        unpack(h, rb_s, 1, order[1:3])
+        to_mate(h, 1)
+        to_mate(h, 2)
+        first(h, base + order[1])
+        first(h, base + order[2])
+        there = base + order[3]
+        wait_bytes(xg_s.at[there, h], qr_sem.at[h])
+        to_mate(h, 3)
+        first(h, there)
+        for k in range(1, 4):
+            from_mate(h, k)
+
+    def middle(h):
+        def some_rows(n, carry):
+            rows = pl.ds(pl.multiple_of(n * 96, 96), 96)
+            gate = gu_acc[rows, 0:FH]
+            up = gu_acc[rows, FH : 2 * FH]
+            sig = jax.nn.sigmoid(gate)
+            act = gate * sig
+            if h == 0:
+                hid_s[rows, :] = (act * up).astype(BF)
+                return carry
+            dh = dh_acc[rows, :]
+            slope = sig * (1.0 + gate * (1.0 - sig))
+            dgu_s[rows, 0:FH] = (dh * up * slope).astype(BF)
+            dgu_s[rows, FH : 2 * FH] = (dh * act).astype(BF)
+            return carry
+
+        lax.fori_loop(0, ROWS // 96, some_rows, 0)
+
+    back = ((0, 1, 2, 3), (3 - y, 0, 1, 2 + y))
+
+    def second(a, j):
+        if a == 0:
+            return dot(hid_s[...], dn_s[j])
+        return dot_nt(dgu_s[...], gu_s[j])
+
+    def for_mate(a, k):
+        t = 4 * a + k
+        xo_s[t] = second(a, far + back[a][k]).astype(BF)
+        pltpu.make_async_remote_copy(
+            xo_s.at[t], xi_s.at[t], xs_sem.at[t], xr_sem.at[t],
+            device_id=(f, mate), device_id_type=MESH,
+        ).start()
+
+    def chip_sum(a, k):
+        t = 4 * a + k
+        own = second(a, base + back[a][k])
+        wait_bytes(xi_s.at[t], xr_sem.at[t])
+        return own + xi_s[t].astype(F32)
+
+    def send_back(t):
+        def some_rows(g, carry):
+            some = v_s[pl.ds(pl.multiple_of(g * MSG, MSG), MSG), :]
+            for s in range(4):
+                sr_s[t, g * 4 + s] = to_message(some, s).astype(BF)
+            return carry
+
+        lax.fori_loop(0, SRC // 4, some_rows, 0)
+
+        def one(i, carry):
+            f2 = spread(i, f)
+            pltpu.make_async_remote_copy(
+                sr_s.at[t, f2], rr_s.at[t, f], s2_sem.at[t], r2_sem.at[t],
+                device_id=(f2, crossed(f2)), device_id_type=MESH,
+            ).start()
+            return carry
+
+        lax.fori_loop(1, SRC, one, 0)
+        pltpu.make_async_copy(sr_s.at[t, f], rr_s.at[t, f], l2_sem.at[t]).start()
+
+    def returned(a, k):
+        v_s[...] = chip_sum(a, k)
+        send_back(3 * a + k)
+
+    def for_other():
+        same = lax.rem(over_cap(iota((ROWS, W), 0)) + f, 2) == 0
+        a, b = chip_sum(1, 0), chip_sum(1, 3)
+        yo_s[...] = jnp.where(same, a, b).astype(BF)
+        vq_s[...] = jnp.where(same, b, a)
+        pltpu.make_async_remote_copy(
+            yo_s, yi_s, ys_sem, yr_sem, device_id=(f, other), device_id_type=MESH
+        ).start()
+
+    def both_chips():
+        wait_bytes(yi_s, yr_sem)
+        v_s[...] = vq_s[...] + yi_s[...].astype(F32)
+        send_back(6)
+
+    def grads(j, carry):
+        for n in range(3):
+            some = slice(n * 256, (n + 1) * 256)
+            gu_s[j, :, some] = dot_tn(xg_s[j, 0], dgu_s[:, some]).astype(BF)
+        dn_s[j] = dot_tn(hid_s[...], xg_s[j, 1]).astype(BF)
+        return carry
+
+    def landed(t):
+        wait_bytes(rr_s.at[t, pl.ds(0, SRC - 1)], r2_sem.at[t])
+        pltpu.make_async_copy(sr_s.at[t, f], rr_s.at[t, f], l2_sem.at[t]).wait()
+
+        def some_rows(g, carry):
+            rows = pl.ds(pl.multiple_of(g * MSG, MSG), MSG)
+            msgs = rr_s[t, pl.ds(g * 4, 4)].astype(F32)
+            for q in range(4):
+                u_s[t, rows, q * Q : (q + 1) * Q] = from_messages(msgs, q).astype(BF)
+            return carry
+
+        lax.fori_loop(0, SRC // 4, some_rows, 0)
+
+    def combined(t):
+        u = u_s[t]
+        if t >= 4:
+            return dot(et_s[...], u).astype(BF)
+        return (dot(whi_s[...], u) + dot(wlo_s[...], u)).astype(BF)
+
+    def share_partial(n):
+        for k in range(2):
+            landed(2 * n + k)
+            po_s[n, k] = combined(2 * n + k)
+        pltpu.make_async_remote_copy(
+            po_s.at[n], pi_s.at[n], ps_sem.at[n], pr_sem.at[n],
+            device_id=(f, other), device_id_type=MESH,
+        ).start()
+
+    def share_whole():
+        n = base + 2 + y
+        landed(6)
+        mq_s[1, n] = combined(6)
+        pltpu.make_async_remote_copy(
+            mq_s.at[1, n], mq_s.at[1, n], ps_sem.at[3], pr_sem.at[3],
+            device_id=(f, other), device_id_type=MESH,
+        ).start()
+
+    def hand_over(n):
+        some = pl.ds(base + 2 * (n % 2), 2)
+        pltpu.make_async_remote_copy(
+            mq_s.at[n // 2, some], mq_s.at[n // 2, some], ms_sem.at[n], mr_sem.at[n],
+            device_id=(f, mate), device_id_type=MESH,
+        ).start()
+
+    def add_partial(n):
+        wait_bytes(pi_s.at[n], pr_sem.at[n])
+        some = pl.ds(base + 2 * (n % 2), 2)
+        mq_s[n // 2, some] = (po_s[n].astype(F32) + pi_s[n].astype(F32)).astype(BF)
+        hand_over(n)
+
+    def pass_whole():
+        wait_bytes(mq_s.at[1, base + 3 - y], pr_sem.at[3])
+        hand_over(3)
+
+    def sum_route(n, device):
+        copy = pltpu.make_async_remote_copy(
+            dr_s.at[2 * n], dr_s.at[2 * n + 1], ds_sem.at[n], dr_sem.at[n],
+            device_id=(f, device), device_id_type=MESH,
+        )
+        copy.start()
+        return copy
+
+    get_one(0)
+    keep_two(0)
+    pack_two(1)
+    get_one(1)
+    keep_two(1)
 
     gu_acc[...] = jnp.zeros_like(gu_acc)
     dh_acc[...] = jnp.zeros_like(dh_acc)
@@ -255,237 +484,32 @@
     wait_bytes(gu_s, w_sem.at[0])
     wait_bytes(dn_s, w_sem.at[1])
 
-    def first(h, j):
-        if h == 1:
-            dh_acc[...] += dot_nt(xg_s[j, 1], dn_s[j])
-            return
-        for n in range(3):
-            cols = slice(n * 256, (n + 1) * 256)
-            gu_acc[:, cols] += dot(xg_s[j, 0], gu_s[j, :, cols])
-
-    order = (2 + y, 0, 1, 3 - y)
-    base = c * NP
-    far = (1 - c) * NP
-
-    def unpack(h, msgs, n, pieces):
-        wait_bytes(msgs.at[h, pl.ds(0, SRC - 1)], rsem.at[2 * n + h])
-        sent = (sq_s, sb_s)[n]
-        pltpu.make_async_copy(sent.at[h, f], msgs.at[h, f], lsem.at[2 * n + h]).wait()
-
-        def some_rows(g, carry):
-            rows = pl.ds(pl.multiple_of(g * MSG, MSG), MSG)
-            some = msgs[h, pl.ds(g * 4, 4)].astype(F32)
-            for at, piece in enumerate(pieces):
-                part = some[:, at * MSG : (at + 1) * MSG, :]
-                for q in range(4):
-                    xg_s[base + piece, h, rows, q * Q : (q + 1) * Q] = from_messages(part, q).astype(BF)
-            return carry
-
-        lax.fori_loop(0, SRC // 4, some_rows, 0)
-
-    def to_mate(h, k):
-        j = base + order[k]
-        pltpu.make_async_remote_copy(
-            xg_s.at[j, h], xg_s.at[j, h], fs_sem.at[4 * h + k], fr_sem.at[4 * h + k],
-            device_id=(f, mate), device_id_type=MESH,
-        ).start()
-
-    def from_mate(h, k):
-        j = far + order[k]
-        wait_bytes(xg_s.at[j, h], fr_sem.at[4 * h + k])
-        first(h, j)
-
-    def get_one(h):
-        j = base + order[0]
-        unpack(h, rq_s, 0, order[0:1])
-        pltpu.make_async_remote_copy(
-            xg_s.at[j, h], xg_s.at[j, h], qs_sem.at[h], qr_sem.at[h],
-            device_id=(f, other), device_id_type=MESH,
-        ).start()
-        to_mate(h, 0)
-
-    def get_rest(h):
-        first(h, base + order[0])
-        from_mate(h, 0)
-        unpack(h, rb_s, 1, order[1:3])
-        to_mate(h, 1)
-        to_mate(h, 2)
-        first(h, base + order[1])
-        first(h, base + order[2])
-        there = base + order[3]
-        wait_bytes(xg_s.at[there, h], qr_sem.at[h])
-        to_mate(h, 3)
-        first(h, there)
-        for k in range(1, 4):
-            from_mate(h, k)
-
-    def middle(h):
-        def some_rows(n, carry):
-            rows = pl.ds(pl.multiple_of(n * 96, 96), 96)
-            gate = gu_acc[rows, 0:FH]
-            up = gu_acc[rows, FH : 2 * FH]
-            sig = jax.nn.sigmoid(gate)
-            act = gate * sig
-            if h == 0:
-                hid_s[rows, :] = (act * up).astype(BF)
-                return carry
-            dh = dh_acc[rows, :]
-            slope = sig * (1.0 + gate * (1.0 - sig))
-            dgu_s[rows, 0:FH] = (dh * up * slope).astype(BF)
-            dgu_s[rows, FH : 2 * FH] = (dh * act).astype(BF)
-            return carry
-
-        lax.fori_loop(0, ROWS // 96, some_rows, 0)
-
-    back = ((0, 1, 2, 3), (3 - y, 0, 1, 2 + y))
-
-    def second(a, j):
-        if a == 0:
-            return dot(hid_s[...], dn_s[j])
-        return dot_nt(dgu_s[...], gu_s[j])
-
-    def for_mate(a, k):
-        t = 4 * a + k
-        xo_s[t] = second(a, far + back[a][k]).astype(BF)
-        pltpu.make_async_remote_copy(
-            xo_s.at[t], xi_s.at[t], xs_sem.at[t], xr_sem.at[t],
-            device_id=(f, mate), device_id_type=MESH,
-        ).start()
-
-    def chip_sum(a, k):
-        t = 4 * a + k
-        own = second(a, base + back[a][k])
-        wait_bytes(xi_s.at[t], xr_sem.at[t])
-        return own + xi_s[t].astype(F32)
-
-    def send_back(t):
-        def some_rows(g, carry):
-            some = v_s[pl.ds(pl.multiple_of(g * MSG, MSG), MSG), :]
-            for s in range(4):
-                sr_s[t, g * 4 + s] = to_message(some, s).astype(BF)
-            return carry
-
-        lax.fori_loop(0, SRC // 4, some_rows, 0)
-
-        def one(i, carry):
-            f2 = spread(i, f)
-            pltpu.make_async_remote_copy(
-                sr_s.at[t, f2], rr_s.at[t, f], s2_sem.at[t], r2_sem.at[t],
-                device_id=(f2, crossed(f2)), device_id_type=MESH,
-            ).start()
-            return carry
-
-        lax.fori_loop(1, SRC, one, 0)
-        pltpu.make_async_copy(sr_s.at[t, f], rr_s.at[t, f], l2_sem.at[t]).start()
-
-    def returned(a, k):
-        v_s[...] = chip_sum(a, k)
-        send_back(3 * a + k)
-
-    def for_other():
-        same = lax.rem(over_cap(iota((ROWS, W), 0)) + f, 2) == 0
-        a, b = chip_sum(1, 0), chip_sum(1, 3)
-        yo_s[...] = jnp.where(same, a, b).astype(BF)
-        vq_s[...] = jnp.where(same, b, a)
-        pltpu.make_async_remote_copy(
-            yo_s, yi_s, ys_sem, yr_sem, device_id=(f, other), device_id_type=MESH
-        ).start()
-
-    def both_chips():
-        wait_bytes(yi_s, yr_sem)
-        v_s[...] = vq_s[...] + yi_s[...].astype(F32)
-        send_back(6)
-
-    def grads(j, carry):
-        for n in range(3):
-            some = slice(n * 256, (n + 1) * 256)
-            gu_s[j, :, some] = dot_tn(xg_s[j, 0], dgu_s[:, some]).astype(BF)
-        dn_s[j] = dot_tn(hid_s[...], xg_s[j, 1]).astype(BF)
-        return carry
-
-    def landed(t):
-        wait_bytes(rr_s.at[t, pl.ds(0, SRC - 1)], r2_sem.at[t])
-        pltpu.make_async_copy(sr_s.at[t, f], rr_s.at[t, f], l2_sem.at[t]).wait()
-
-        def some_rows(g, carry):
-            rows = pl.ds(pl.multiple_of(g * MSG, MSG), MSG)
-            msgs = rr_s[t, pl.ds(g * 4, 4)].astype(F32)
-            for q in range(4):
-                u_s[t, rows, q * Q : (q + 1) * Q] = from_messages(msgs, q).astype(BF)
-            return carry
-
-        lax.fori_loop(0, SRC // 4, some_rows, 0)
-
-    def combined(t):
-        u = u_s[t]
-        if t >= 4:
-            return dot(et_s[...], u).astype(BF)
-        return (dot(whi_s[...], u) + dot(wlo_s[...], u)).astype(BF)
-
-    def share_partial(n):
-        for k in range(2):
-            landed(2 * n + k)
-            po_s[n, k] = combined(2 * n + k)
-        pltpu.make_async_remote_copy(
-            po_s.at[n], pi_s.at[n], ps_sem.at[n], pr_sem.at[n],
-            device_id=(f, other), device_id_type=MESH,
-        ).start()
-
-    def share_whole():
-        n = base + 2 + y
-        landed(6)
-        mq_s[1, n] = combined(6)
-        pltpu.make_async_remote_copy(
-            mq_s.at[1, n], mq_s.at[1, n], ps_sem.at[3], pr_sem.at[3],
-            device_id=(f, other), device_id_type=MESH,
-        ).start()
-
-    def hand_over(n):
-        some = pl.ds(base + 2 * (n % 2), 2)
-        pltpu.make_async_remote_copy(
-            mq_s.at[n // 2, some], mq_s.at[n // 2, some], ms_sem.at[n], mr_sem.at[n],
-            device_id=(f, mate), device_id_type=MESH,
-        ).start()
-
-    def add_partial(n):
-        wait_bytes(pi_s.at[n], pr_sem.at[n])
-        some = pl.ds(base + 2 * (n % 2), 2)
-        mq_s[n // 2, some] = (po_s[n].astype(F32) + pi_s[n].astype(F32)).astype(BF)
-        hand_over(n)
-
-    def pass_whole():
-        wait_bytes(mq_s.at[1, base + 3 - y], pr_sem.at[3])
-        hand_over(3)
-
-    def sum_route(n, device):
-        copy = pltpu.make_async_remote_copy(
-            dr_s.at[2 * n], dr_s.at[2 * n + 1], ds_sem.at[n], dr_sem.at[n],
-            device_id=(f, device), device_id_type=MESH,
-        )
-        copy.start()
-        return copy
-
-    get_one(0)
+    use_one(0)
+    use_one(1)
+    two_sent(0)
+    to_all(send_two, 1)
     get_rest(0)
     middle(0)
     for k in range(4):
         for_mate(0, k)
-    get_one(1)
-    for k in range(4):
+    for k in range(3):
         returned(0, k)
     get_rest(1)
     middle(1)
     for k in range(4):
         for_mate(1, k)
     for_other()
+    returned(0, 3)
     returned(1, 1)
     returned(1, 2)
     share_partial(0)
-    prod = dot_nt(dout_v[:, 0:W], u_s[0]) + dot_nt(dout_v[:, W : 2 * W], u_s[1])
-    lax.fori_loop(0, NP, grads, 0)
     both_chips()
     share_partial(1)
-    prod = prod + dot_nt(dout_v[:, 2 * W : 3 * W], u_s[2]) + dot_nt(dout_v[:, 3 * W :], u_s[3])
+    lax.fori_loop(0, NP, grads, 0)
+    share_partial(2)
+    prod = dot_nt(dout_v[:, 0:W], u_s[0])
+    for k in range(1, 4):
+        prod = prod + dot_nt(dout_v[:, k * W : (k + 1) * W], u_s[k])
     kept = jnp.where(et_s[...] > 0, prod, 0.0)
     hi = kept.astype(BF)
     lo = (kept - hi.astype(F32)).astype(BF)
@@ -494,12 +518,11 @@
     route = sum_route(0, other)
     add_partial(0)
     lax.fori_loop(NP, 2 * NP, grads, 0)
-    share_partial(2)
     add_partial(1)
+    share_whole()
     route.wait()
     dr_s[2] = dr_s[0] + dr_s[1]
     route = sum_route(1, mate)
-    share_whole()
     add_partial(2)
     route.wait()
     total = (dr_s[2] + dr_s[3]).T
@@ -510,9 +533,8 @@
     for n in range(4):
         wait_bytes(mq_s.at[n // 2, pl.ds(far + 2 * (n % 2), 2)], mr_sem.at[n])
 
+    two_sent(1)
     for h in range(2):
-        wait_bytes(sq_s.at[h, pl.ds(0, SRC - 1)], ssem.at[h])
-        wait_bytes(sb_s.at[h, pl.ds(0, SRC - 1)], ssem.at[2 + h])
         wait_bytes(xg_s.at[0, 0], qs_sem.at[h])
     for n in range(8):
         wait_bytes(xg_s.at[0, 0], fs_sem.at[n])

time: 94.2 us -> 90.9 us (0.965)
  the two profiles are of different devices: /device:TPU:31 before, /device:TPU:0 now
where the time goes in v4:
time: 90.9 us; the launch traced here: 89.2 us
  Pallas kernels  88.5 us (97%)
    pallas_call x1, Pallas kernels, per_device(): pl.pallas_call(kernel, out_shape=(v((2, 2 * NP, TOK, W), BF), v((top, TOK...  83.4 us
    pallas_call x1, Pallas kernels, per_device(): pl.pallas_call(store_kernel, out_shape=(shape((TOK, D), BF), shape((TOK,...  5.14 us

profile of v4, /device:TPU:0, one launch (start us, length us, event | category | flops | bytes accessed | tf_op | source)
XLA Modules:
  0.0 89.2 jit_solution(15447372322702155206)
XLA Ops:
  0.6 83.4 %shard_map.118 = (bf16[2,8,128,512]{3,2,1,0:T(8,128)(2,1)S(1)}, f32[8,128]{1,0:T(8,128)S(1)}, bf16[8,512,768]{2,1,0:T(8,128)(2,1)S(1)}, bf16[8,384,512]{2,1,0:T(8,128)(2,1)S(1)}) custom-call(s32[8,128]{1,0:T(8,128)} %bitcast.3, f32[8,128]{1,0:T(8,128)} %bitcast.4, bf16[128,4096]{1,0:T(8,128)(2,1)} %tok_hbm.1, bf16[128,4096]{1,0:T(8,128)(2,1)} %dout_hbm.1, ...), custom_call_target="tpu_custom_call" | custom-call | flops 11000000512 | bytes 12000000 | tf_op jit(solution)/shard_map/pallas_call | solution.py:582
  84.0 5.1 %shard_map.119 = (bf16[128,4096]{1,0:T(8,128)(2,1)}, bf16[128,4096]{1,0:T(8,128)(2,1)}, f32[8,128]{1,0:T(8,128)}, bf16[1,4096,384]{2,1,0:T(8,128)(2,1)}, bf16[1,...) custom-call(bf16[2,8,128,512]{3,2,1,0:T(8,128)(2,1)S(1)} %get-tuple-element.16.mq_ref, ...), custom_call_target="tpu_custom_call" | custom-call | bytes 12000000 | tf_op jit(solution)/shard_map/pallas_call | solution.py:617

commit v5 on v4

--- a/solution.py
+++ b/solution.py
@@ -496,7 +496,7 @@
         returned(0, k)
     get_rest(1)
     middle(1)
-    for k in range(4):
+    for k in (0, 3, 1, 2):
         for_mate(1, k)
     for_other()
     returned(0, 3)

time: 90.9 us -> 90.1 us (level)
  no operation moved by 1% of the time
where the time goes in v5:
time: 90.1 us; the launch traced here: 88.5 us
  Pallas kernels  87.9 us (98%)
    pallas_call x1, Pallas kernels, per_device(): pl.pallas_call(kernel, out_shape=(v((2, 2 * NP, TOK, W), BF), v((top, TOK...  82.7 us
    pallas_call x1, Pallas kernels, per_device(): pl.pallas_call(store_kernel, out_shape=(shape((TOK, D), BF), shape((TOK,...  5.14 us

profile of v5, /device:TPU:0, one launch (start us, length us, event | category | flops | bytes accessed | tf_op | source)
XLA Modules:
  0.0 88.5 jit_solution(4737859698359838799)
XLA Ops:
  0.6 82.7 %shard_map.118 = (bf16[2,8,128,512]{3,2,1,0:T(8,128)(2,1)S(1)}, f32[8,128]{1,0:T(8,128)S(1)}, bf16[8,512,768]{2,1,0:T(8,128)(2,1)S(1)}, bf16[8,384,512]{2,1,0:T(8,128)(2,1)S(1)}) custom-call(s32[8,128]{1,0:T(8,128)} %bitcast.3, f32[8,128]{1,0:T(8,128)} %bitcast.4, bf16[128,4096]{1,0:T(8,128)(2,1)} %tok_hbm.1, bf16[128,4096]{1,0:T(8,128)(2,1)} %dout_hbm.1, ...), custom_call_target="tpu_custom_call" | custom-call | flops 11000000512 | bytes 12000000 | tf_op jit(solution)/shard_map/pallas_call | solution.py:582
  83.4 5.1 %shard_map.119 = (bf16[128,4096]{1,0:T(8,128)(2,1)}, bf16[128,4096]{1,0:T(8,128)(2,1)}, f32[8,128]{1,0:T(8,128)}, bf16[1,4096,384]{2,1,0:T(8,128)(2,1)}, bf16[1,...) custom-call(bf16[2,8,128,512]{3,2,1,0:T(8,128)(2,1)S(1)} %get-tuple-element.16.mq_ref, ...), custom_call_target="tpu_custom_call" | custom-call | bytes 12000000 | tf_op jit(solution)/shard_map/pallas_call | solution.py:617
